TPU v7x, 256 devices: a whole 4x4x8 slice. The times are simulated.
256 devices in a mesh: chain: 16 (over y, x), sector: 16 (over z, core).
Axes of the slice: x: 4, y: 4, z: 8, core: 2. Of those that a mesh axis runs over, the one named last changes fastest.
Arguments:
- left_edge: float32 [16, 14, 128, 128], P('sector'), may hold values from -0.5 to 0.5
- transfer: float32 [16, 16, 128, 128], P('chain', 'sector'), may hold values from -0.078125 to 0.078125
- completed: float32 [16, 16, 14, 128, 128], P('chain', 'sector'), may hold values from -0.25 to 0.25
- right_env: bfloat16 [16, 16, 14, 128, 128], P('chain', 'sector'), may hold values from -0.5 to 0.5
- psi_init: bfloat16 [16, 16, 16, 128, 128], P('chain', 'sector'), may hold values from -6 to 6
- mpo: bfloat16 [14, 16, 16, 14], replicated, may hold values from -0.75 to 0.75
- mpo_mask: int32 [14, 14], replicated, may hold values 0 or 1
- charge_shift: int32 [16, 16], P('sector'), may hold values from -1 to 1
- block_size: int32 [16], replicated, may hold values from 1 to 128, 1536 in all
Outputs:
- psi_out: bfloat16 [16, 16, 16, 128, 128], P('chain', 'sector')
- energy: float32 [16], P('chain')
Inputs may be any that keep to these rules, and one draw needn't show every extreme that they name: `block_size`: some block has 128 live rows.
All inputs are finite; a program needn't handle non-finite values.
Results may differ from a plain program's by a relative error of at most 0.024.
Values may be sent and summed in bfloat16 or wider, within the bound.
No kernel may reach another device: no remote copies, remote signals or barrier semaphores. Data moves between devices by JAX's collectives and lax.ppermute only.
A program may use at most 128 MiB of HBM per device.

v0:
```python
import jax
import jax.numpy as jnp
from jax import lax
from jax.sharding import PartitionSpec as P

ITERS = 3


carry_weight = 0.8
step_size = 0.5


def from_behind(block, axis, distance):
    devices = range(lax.axis_size(axis))
    route = [(i - distance, i) for i in devices if i - distance in devices]
    return lax.ppermute(block, axis, route)


def extended_2(shard, sides, width):
    for axis, dim in sides:
        size, length = (lax.axis_size(axis), shard.shape[dim])
        up = [(i, (i + 1) % size) for i in range(size - 1)]
        down = [(j, i) for i, j in up]
        last = lax.slice_in_dim(shard, length - width, length, axis=dim)
        first = lax.slice_in_dim(shard, 0, width, axis=dim)
        before = lax.ppermute(last, axis, up)
        after = lax.ppermute(first, axis, down)
        shard = jnp.concatenate([before, shard, after], axis=dim)
    return shard


def congruence(matrix, environ):
    inner = jnp.einsum("qwac,qcd->qwad", environ, matrix, precision=lax.Precision.HIGHEST)
    return jnp.einsum("qab,qwad->qwbd", matrix, inner, precision=lax.Precision.HIGHEST)


def body(
    left_edge, transfer, completed, right_env, psi_init, mpo, mpo_mask, charge_shift, block_size
):
    sec_local = left_edge.shape[0]
    rows = left_edge.shape[2]
    total_sec = block_size.shape[0]
    identity = jnp.eye(rows, dtype=jnp.float32)
    own_map = carry_weight * identity[None] + transfer[0]
    own_add = completed[0]
    chain_pos = lax.axis_index("chain")

    def advance(turn, incoming):
        outgoing = congruence(own_map, incoming) + own_add
        received = from_behind(outgoing.astype(jnp.bfloat16), "chain", 1).astype(outgoing.dtype)
        return jnp.where(chain_pos == 0, left_edge, received)

    environ = lax.fori_loop(0, lax.axis_size("chain") - 1, advance, left_edge)
    sector_first = lax.axis_index("sector") * sec_local
    sector_ids = sector_first + jnp.arange(sec_local, dtype=jnp.int32)
    target = sector_ids[:, None] + charge_shift
    valid = (target >= 0) & (target < total_sec)
    clipped = jnp.clip(target, 0, total_sec - 1)
    local_pick = jnp.clip(target - sector_first + 1, 0, sec_local + 1)
    row_ids = jnp.arange(rows, dtype=jnp.int32)
    left_live = row_ids[None, :] < block_size[sector_ids][:, None]
    right_live = row_ids[None, None, :] < block_size[clipped][:, :, None]
    mask = (
        valid[:, :, None, None] & left_live[:, None, :, None] & right_live[:, :, None, :]
    ).astype(jnp.float32)
    allowed = (charge_shift[:, :, None] == charge_shift[:, None, :]).astype(jnp.float32)
    operator = (
        mpo.astype(jnp.float32)[None]
        * mpo_mask.astype(jnp.float32)[None, :, None, None, :]
        * allowed[:, None, :, :, None]
    ).astype(jnp.bfloat16)
    extended = extended_2(right_env[0], (("sector", 0),), 1)
    chosen = jnp.take(extended, local_pick, axis=0)
    env_bf = environ.astype(jnp.bfloat16)
    tensor = mask * psi_init[0].astype(jnp.float32)
    rayleigh = jnp.float32(0.0)
    for step in range(ITERS):
        first = jnp.einsum(
            "qwae,qped->qpwad",
            env_bf,
            tensor.astype(jnp.bfloat16),
            preferred_element_type=jnp.float32,
        ).astype(jnp.bfloat16)
        second = jnp.einsum(
            "qwpxv,qxwad->qpvad", operator, first, preferred_element_type=jnp.float32
        ).astype(jnp.bfloat16)
        image = (
            jnp.einsum("qpvad,qpvbd->qpab", second, chosen, preferred_element_type=jnp.float32)
            * mask
        )
        norm_sq, intersection = lax.psum(
            (jnp.sum(tensor * tensor), jnp.sum(tensor * image)), "sector"
        )
        rayleigh = intersection / norm_sq
        updated = tensor - step_size * (image - rayleigh * tensor)
        new_sq = lax.psum(jnp.sum(updated * updated), "sector")
        tensor = updated / jnp.sqrt(new_sq)
    return (tensor.astype(jnp.bfloat16)[None], jnp.reshape(rayleigh, (1,)))


def solution(mesh):
    placed = (
        P("sector", None, None, None),
        P("chain", "sector", None, None),
        P("chain", "sector", None, None, None),
        P("chain", "sector", None, None, None),
        P("chain", "sector", None, None, None),
        P(),
        P(),
        P("sector", None),
        P(),
    )
    return jax.shard_map(
        body,
        mesh=mesh,
        in_specs=placed,
        out_specs=(P("chain", "sector", None, None, None), P("chain")),
        check_vma=False,
    )
```

profile of v0, /device:TPU:25, one launch (start us, length us, event | category | flops | bytes accessed | tf_op | source)
XLA Modules:
  0.0 535.6 jit_solution(15179224230695428214)
XLA Ops:
  18.4 230.0 %while.13 = (s32[]{:T(128)}, f32[1,14,128,128]{2,3,1,0:T(8,128)S(1)}, pred[]{:T(512)}, f32[1,128,128]{2,1,0:T(8,128)S(1)}, f32[1,14,128,128]{2,3,1,0:T(8,128)S(1)}, /*index=5*/f32[1,14,128,128]{2,3,1,0:T(8,128)S(1)}, s32[]{:T(128)}) while((s32[]{:T(128)}, f32[1,14,128,128]{2,3,1,0:T(8,128)S(1)}, pred[]{:T(512)}, f32[1,128,128]{2,1,0:T(8,128)S(1)}, ...), condition=%wide.region_1.2_spmd, body=%wide.region_0.1_spmd.sunk | while | flops 705560576 | bytes 8388726 | solution.py:53
  23.4 13.2 %collective-permute-done = bf16[1,14,128,128]{2,3,1,0:T(8,128)(2,1)S(1)} collective-permute-done((bf16[1,14,128,128]{2,3,1,0:T(8,128)(2,1)S(1)}, bf16[1,14,128,128]{2,3,1,0:T(8,128)(2,1)S(1)}, u32[]{:S(2)}, u32[]{:S(2)}) %collective-permute-start) | collective-permute-done | bytes 458784 | tf_op jit(solution)/shard_map/while/body/eval_jaxpr/ppermute | solution.py:16
  40.5 13.6 %collective-permute-done = bf16[1,14,128,128]{2,3,1,0:T(8,128)(2,1)S(1)} collective-permute-done((bf16[1,14,128,128]{2,3,1,0:T(8,128)(2,1)S(1)}, bf16[1,14,128,128]{2,3,1,0:T(8,128)(2,1)S(1)}, u32[]{:S(2)}, u32[]{:S(2)}) %collective-permute-start) | collective-permute-done | bytes 458784 | tf_op jit(solution)/shard_map/while/body/eval_jaxpr/ppermute | solution.py:16
  57.9 12.6 %collective-permute-done = bf16[1,14,128,128]{2,3,1,0:T(8,128)(2,1)S(1)} collective-permute-done((bf16[1,14,128,128]{2,3,1,0:T(8,128)(2,1)S(1)}, bf16[1,14,128,128]{2,3,1,0:T(8,128)(2,1)S(1)}, u32[]{:S(2)}, u32[]{:S(2)}) %collective-permute-start) | collective-permute-done | bytes 458784 | tf_op jit(solution)/shard_map/while/body/eval_jaxpr/ppermute | solution.py:16
  74.4 11.7 %collective-permute-done = bf16[1,14,128,128]{2,3,1,0:T(8,128)(2,1)S(1)} collective-permute-done((bf16[1,14,128,128]{2,3,1,0:T(8,128)(2,1)S(1)}, bf16[1,14,128,128]{2,3,1,0:T(8,128)(2,1)S(1)}, u32[]{:S(2)}, u32[]{:S(2)}) %collective-permute-start) | collective-permute-done | bytes 458784 | tf_op jit(solution)/shard_map/while/body/eval_jaxpr/ppermute | solution.py:16
  90.0 10.8 %collective-permute-done = bf16[1,14,128,128]{2,3,1,0:T(8,128)(2,1)S(1)} collective-permute-done((bf16[1,14,128,128]{2,3,1,0:T(8,128)(2,1)S(1)}, bf16[1,14,128,128]{2,3,1,0:T(8,128)(2,1)S(1)}, u32[]{:S(2)}, u32[]{:S(2)}) %collective-permute-start) | collective-permute-done | bytes 458784 | tf_op jit(solution)/shard_map/while/body/eval_jaxpr/ppermute | solution.py:16
  104.6 9.9 %collective-permute-done = bf16[1,14,128,128]{2,3,1,0:T(8,128)(2,1)S(1)} collective-permute-done((bf16[1,14,128,128]{2,3,1,0:T(8,128)(2,1)S(1)}, bf16[1,14,128,128]{2,3,1,0:T(8,128)(2,1)S(1)}, u32[]{:S(2)}, u32[]{:S(2)}) %collective-permute-start) | collective-permute-done | bytes 458784 | tf_op jit(solution)/shard_map/while/body/eval_jaxpr/ppermute | solution.py:16
  171.5 10.1 %collective-permute-done = bf16[1,14,128,128]{2,3,1,0:T(8,128)(2,1)S(1)} collective-permute-done((bf16[1,14,128,128]{2,3,1,0:T(8,128)(2,1)S(1)}, bf16[1,14,128,128]{2,3,1,0:T(8,128)(2,1)S(1)}, u32[]{:S(2)}, u32[]{:S(2)}) %collective-permute-start) | collective-permute-done | bytes 458784 | tf_op jit(solution)/shard_map/while/body/eval_jaxpr/ppermute | solution.py:16
  185.5 11.2 %collective-permute-done = bf16[1,14,128,128]{2,3,1,0:T(8,128)(2,1)S(1)} collective-permute-done((bf16[1,14,128,128]{2,3,1,0:T(8,128)(2,1)S(1)}, bf16[1,14,128,128]{2,3,1,0:T(8,128)(2,1)S(1)}, u32[]{:S(2)}, u32[]{:S(2)}) %collective-permute-start) | collective-permute-done | bytes 458784 | tf_op jit(solution)/shard_map/while/body/eval_jaxpr/ppermute | solution.py:16
  200.5 12.3 %collective-permute-done = bf16[1,14,128,128]{2,3,1,0:T(8,128)(2,1)S(1)} collective-permute-done((bf16[1,14,128,128]{2,3,1,0:T(8,128)(2,1)S(1)}, bf16[1,14,128,128]{2,3,1,0:T(8,128)(2,1)S(1)}, u32[]{:S(2)}, u32[]{:S(2)}) %collective-permute-start) | collective-permute-done | bytes 458784 | tf_op jit(solution)/shard_map/while/body/eval_jaxpr/ppermute | solution.py:16
  216.7 13.3 %collective-permute-done = bf16[1,14,128,128]{2,3,1,0:T(8,128)(2,1)S(1)} collective-permute-done((bf16[1,14,128,128]{2,3,1,0:T(8,128)(2,1)S(1)}, bf16[1,14,128,128]{2,3,1,0:T(8,128)(2,1)S(1)}, u32[]{:S(2)}, u32[]{:S(2)}) %collective-permute-start) | collective-permute-done | bytes 458784 | tf_op jit(solution)/shard_map/while/body/eval_jaxpr/ppermute | solution.py:16
  233.9 14.5 %collective-permute-done = bf16[1,14,128,128]{2,3,1,0:T(8,128)(2,1)S(1)} collective-permute-done((bf16[1,14,128,128]{2,3,1,0:T(8,128)(2,1)S(1)}, bf16[1,14,128,128]{2,3,1,0:T(8,128)(2,1)S(1)}, u32[]{:S(2)}, u32[]{:S(2)}) %collective-permute-start) | collective-permute-done | bytes 458784 | tf_op jit(solution)/shard_map/while/body/eval_jaxpr/ppermute | solution.py:16
  255.1 11.0 %copy.32 = bf16[16,14,128,128,1]{3,0,1,2,4:T(8,128)(2,1)} copy(bf16[16,14,128,128,1]{2,3,1,0,4:T(8,128)(2,1)} %convert_bitcast_fusion.2) | data formatting | bytes 14680064 | tf_op jit(solution)/shard_map/reshape.25
  266.1 11.5 %fusion.27 = bf16[16,14,128,128,1]{3,0,4,2,1:T(8,128)(2,1)} fusion(bf16[16,14,128,128,1]{3,0,1,2,4:T(8,128)(2,1)} %copy.32, bf16[14,16,16,14]{2,1,3,0:T(8,128)(2,1)S(1)} %copy-done.8, f32[16,16]{1,0:T(8,128)S(1)} %compare_convert_fusion, f32[14,14]{1,0:T(8,128)S(1)} %copy-done.3), kind=kOutput, calls=%fused_computation.57 | convolution fusion | flops 1644367872 | bytes 14782224 | tf_op jit(solution)/shard_map/qwpxv,qxwad->qpvad/dot_general | solution.py:84
  291.8 40.2 %all-reduce.2 = (f32[]{:T(128)}, f32[]{:T(128)}) all-reduce(f32[]{:T(128)} %get-tuple-element.124, f32[]{:T(128)} %fusion.21), channel_id=1, replica_groups=mesh['chain'=16,'sector'=16] {'sector'}, use_global_device_ids=true, to_apply=%region_3.4 | all-reduce | flops 2 | bytes 16 | tf_op jit(solution)/shard_map/psum | solution.py:91
  334.5 23.9 %psum.65 = f32[]{:T(128)} all-reduce(f32[]{:T(128)} %multiply_reduce_fusion.6), channel_id=1, replica_groups=mesh['chain'=16,'sector'=16] {'sector'}, use_global_device_ids=true, to_apply=%region_7.8 | all-reduce | flops 1 | bytes 8 | tf_op jit(solution)/shard_map/psum | solution.py:96
  364.6 10.9 %copy.37 = bf16[16,14,128,128,1]{3,0,1,2,4:T(8,128)(2,1)} copy(bf16[16,14,128,128,1]{2,3,1,0,4:T(8,128)(2,1)} %convert_bitcast_fusion.1) | data formatting | bytes 14680064 | tf_op jit(solution)/shard_map/reshape.36
  375.5 11.4 %fusion.25 = bf16[16,14,128,128,1]{3,0,4,2,1:T(8,128)(2,1)} fusion(bf16[16,14,128,128,1]{3,0,1,2,4:T(8,128)(2,1)} %copy.37, bf16[14,16,16,14]{2,1,3,0:T(8,128)(2,1)S(1)} %copy-done.9, f32[16,16]{1,0:T(8,128)S(1)} %compare_convert_fusion, f32[14,14]{1,0:T(8,128)S(1)} %copy-done.4), kind=kOutput, calls=%fused_computation.55 | convolution fusion | flops 1644367872 | bytes 14782224 | tf_op jit(solution)/shard_map/qwpxv,qxwad->qpvad/dot_general | solution.py:84
  394.3 24.5 %all-reduce.1 = (f32[]{:T(128)}, f32[]{:T(128)}) all-reduce(f32[]{:T(128)} %get-tuple-element.101, f32[]{:T(128)} %get-tuple-element.100), channel_id=1, replica_groups=mesh['chain'=16,'sector'=16] {'sector'}, use_global_device_ids=true, to_apply=%region_9.10 | all-reduce | flops 2 | bytes 16 | tf_op jit(solution)/shard_map/psum | solution.py:91
  421.0 24.4 %psum.68 = f32[]{:T(128)} all-reduce(f32[]{:T(128)} %multiply_reduce_fusion.3), channel_id=1, replica_groups=mesh['chain'=16,'sector'=16] {'sector'}, use_global_device_ids=true, to_apply=%region_13.14 | all-reduce | flops 1 | bytes 8 | tf_op jit(solution)/shard_map/psum | solution.py:96
  452.5 10.9 %copy.42 = bf16[16,14,128,128,1]{3,0,1,2,4:T(8,128)(2,1)} copy(bf16[16,14,128,128,1]{2,3,1,0,4:T(8,128)(2,1)} %convert_bitcast_fusion) | data formatting | bytes 14680064 | tf_op jit(solution)/shard_map/reshape.45
  463.4 11.4 %fusion.23 = bf16[16,14,128,128,1]{3,0,4,2,1:T(8,128)(2,1)} fusion(bf16[16,14,128,128,1]{3,0,1,2,4:T(8,128)(2,1)} %copy.42, bf16[14,16,16,14]{2,1,3,0:T(8,128)(2,1)S(1)} %copy-done.10, f32[16,16]{1,0:T(8,128)S(1)} %compare_convert_fusion, f32[14,14]{1,0:T(8,128)S(1)} %copy-done.4), kind=kOutput, calls=%fused_computation.53 | convolution fusion | flops 1644367872 | bytes 14782224 | tf_op jit(solution)/shard_map/qwpxv,qxwad->qpvad/dot_general | solution.py:84
  482.2 24.2 %all-reduce = (f32[]{:T(128)}, f32[]{:T(128)}) all-reduce(f32[]{:T(128)} %get-tuple-element.99, f32[]{:T(128)} %get-tuple-element.98), channel_id=1, replica_groups=mesh['chain'=16,'sector'=16] {'sector'}, use_global_device_ids=true, to_apply=%region_15.16 | all-reduce | flops 2 | bytes 16 | tf_op jit(solution)/shard_map/psum | solution.py:91
  508.6 24.2 %psum.71 = f32[]{:T(128)} all-reduce(f32[]{:T(128)} %multiply_reduce_fusion), channel_id=1, replica_groups=mesh['chain'=16,'sector'=16] {'sector'}, use_global_device_ids=true, to_apply=%region_19.20 | all-reduce | flops 1 | bytes 8 | tf_op jit(solution)/shard_map/psum | solution.py:96
  (119 shorter events, 165.6 us)
Async XLA Ops:
  0.6 278.0 %collective-permute-start.2 = (bf16[1,14,128,128]{3,2,1,0:T(8,128)(2,1)}, bf16[1,14,128,128]{3,2,1,0:T(8,128)(2,1)}, u32[]{:S(2)}, u32[]{:S(2)}) collective-permute-start(bf16[1,14,128,128]{3,2,1,0:T(8,128)(2,1)} %bitcast.183), channel_id=1, source_target_pairs={{1,0},{2,1},{3,2},{4,3},{5,4},{6,5},{7,6},{8,7},{9,8},{10,9},{11,1... | collective-permute-start | bytes 1376264 | tf_op jit(solution)/shard_map/ppermute | solution.py:27
  3.2 275.4 %collective-permute-start.1 = (bf16[1,14,128,128]{3,2,1,0:T(8,128)(2,1)}, bf16[1,14,128,128]{3,2,1,0:T(8,128)(2,1)}, u32[]{:S(2)}, u32[]{:S(2)}) collective-permute-start(bf16[1,14,128,128]{3,2,1,0:T(8,128)(2,1)} %bitcast.184), channel_id=1, source_target_pairs={{0,1},{1,2},{2,3},{3,4},{4,5},{5,6},{6,7},{7,8},{8,9},{9,10},{10,1... | collective-permute-start | bytes 1376264 | tf_op jit(solution)/shard_map/ppermute | solution.py:26
  20.3 16.3 %collective-permute-start = (bf16[1,14,128,128]{2,3,1,0:T(8,128)(2,1)S(1)}, bf16[1,14,128,128]{2,3,1,0:T(8,128)(2,1)S(1)}, u32[]{:S(2)}, u32[]{:S(2)}) collective-permute-start(bf16[1,14,128,128]{2,3,1,0:T(8,128)(2,1)S(1)} %fusion.69), channel_id=1, source_target_pairs={{0,16},{16,32},{32,48},{48,64},{64,80},{80,96},{96,112},{112,128},... | collective-permute-start | bytes 1376264 | tf_op jit(solution)/shard_map/while/body/eval_jaxpr/ppermute | solution.py:16
  38.5 15.5 %collective-permute-start = (bf16[1,14,128,128]{2,3,1,0:T(8,128)(2,1)S(1)}, bf16[1,14,128,128]{2,3,1,0:T(8,128)(2,1)S(1)}, u32[]{:S(2)}, u32[]{:S(2)}) collective-permute-start(bf16[1,14,128,128]{2,3,1,0:T(8,128)(2,1)S(1)} %fusion.69), channel_id=1, source_target_pairs={{0,16},{16,32},{32,48},{48,64},{64,80},{80,96},{96,112},{112,128},... | collective-permute-start | bytes 1376264 | tf_op jit(solution)/shard_map/while/body/eval_jaxpr/ppermute | solution.py:16
  56.0 14.6 %collective-permute-start = (bf16[1,14,128,128]{2,3,1,0:T(8,128)(2,1)S(1)}, bf16[1,14,128,128]{2,3,1,0:T(8,128)(2,1)S(1)}, u32[]{:S(2)}, u32[]{:S(2)}) collective-permute-start(bf16[1,14,128,128]{2,3,1,0:T(8,128)(2,1)S(1)} %fusion.69), channel_id=1, source_target_pairs={{0,16},{16,32},{32,48},{48,64},{64,80},{80,96},{96,112},{112,128},... | collective-permute-start | bytes 1376264 | tf_op jit(solution)/shard_map/while/body/eval_jaxpr/ppermute | solution.py:16
  72.5 13.6 %collective-permute-start = (bf16[1,14,128,128]{2,3,1,0:T(8,128)(2,1)S(1)}, bf16[1,14,128,128]{2,3,1,0:T(8,128)(2,1)S(1)}, u32[]{:S(2)}, u32[]{:S(2)}) collective-permute-start(bf16[1,14,128,128]{2,3,1,0:T(8,128)(2,1)S(1)} %fusion.69), channel_id=1, source_target_pairs={{0,16},{16,32},{32,48},{48,64},{64,80},{80,96},{96,112},{112,128},... | collective-permute-start | bytes 1376264 | tf_op jit(solution)/shard_map/while/body/eval_jaxpr/ppermute | solution.py:16
  88.1 12.7 %collective-permute-start = (bf16[1,14,128,128]{2,3,1,0:T(8,128)(2,1)S(1)}, bf16[1,14,128,128]{2,3,1,0:T(8,128)(2,1)S(1)}, u32[]{:S(2)}, u32[]{:S(2)}) collective-permute-start(bf16[1,14,128,128]{2,3,1,0:T(8,128)(2,1)S(1)} %fusion.69), channel_id=1, source_target_pairs={{0,16},{16,32},{32,48},{48,64},{64,80},{80,96},{96,112},{112,128},... | collective-permute-start | bytes 1376264 | tf_op jit(solution)/shard_map/while/body/eval_jaxpr/ppermute | solution.py:16
  102.7 11.8 %collective-permute-start = (bf16[1,14,128,128]{2,3,1,0:T(8,128)(2,1)S(1)}, bf16[1,14,128,128]{2,3,1,0:T(8,128)(2,1)S(1)}, u32[]{:S(2)}, u32[]{:S(2)}) collective-permute-start(bf16[1,14,128,128]{2,3,1,0:T(8,128)(2,1)S(1)} %fusion.69), channel_id=1, source_target_pairs={{0,16},{16,32},{32,48},{48,64},{64,80},{80,96},{96,112},{112,128},... | collective-permute-start | bytes 1376264 | tf_op jit(solution)/shard_map/while/body/eval_jaxpr/ppermute | solution.py:16
  116.4 11.3 %collective-permute-start = (bf16[1,14,128,128]{2,3,1,0:T(8,128)(2,1)S(1)}, bf16[1,14,128,128]{2,3,1,0:T(8,128)(2,1)S(1)}, u32[]{:S(2)}, u32[]{:S(2)}) collective-permute-start(bf16[1,14,128,128]{2,3,1,0:T(8,128)(2,1)S(1)} %fusion.69), channel_id=1, source_target_pairs={{0,16},{16,32},{32,48},{48,64},{64,80},{80,96},{96,112},{112,128},... | collective-permute-start | bytes 1376264 | tf_op jit(solution)/shard_map/while/body/eval_jaxpr/ppermute | solution.py:16
  129.7 11.3 %collective-permute-start = (bf16[1,14,128,128]{2,3,1,0:T(8,128)(2,1)S(1)}, bf16[1,14,128,128]{2,3,1,0:T(8,128)(2,1)S(1)}, u32[]{:S(2)}, u32[]{:S(2)}) collective-permute-start(bf16[1,14,128,128]{2,3,1,0:T(8,128)(2,1)S(1)} %fusion.69), channel_id=1, source_target_pairs={{0,16},{16,32},{32,48},{48,64},{64,80},{80,96},{96,112},{112,128},... | collective-permute-start | bytes 1376264 | tf_op jit(solution)/shard_map/while/body/eval_jaxpr/ppermute | solution.py:16
  143.0 11.3 %collective-permute-start = (bf16[1,14,128,128]{2,3,1,0:T(8,128)(2,1)S(1)}, bf16[1,14,128,128]{2,3,1,0:T(8,128)(2,1)S(1)}, u32[]{:S(2)}, u32[]{:S(2)}) collective-permute-start(bf16[1,14,128,128]{2,3,1,0:T(8,128)(2,1)S(1)} %fusion.69), channel_id=1, source_target_pairs={{0,16},{16,32},{32,48},{48,64},{64,80},{80,96},{96,112},{112,128},... | collective-permute-start | bytes 1376264 | tf_op jit(solution)/shard_map/while/body/eval_jaxpr/ppermute | solution.py:16
  156.3 11.3 %collective-permute-start = (bf16[1,14,128,128]{2,3,1,0:T(8,128)(2,1)S(1)}, bf16[1,14,128,128]{2,3,1,0:T(8,128)(2,1)S(1)}, u32[]{:S(2)}, u32[]{:S(2)}) collective-permute-start(bf16[1,14,128,128]{2,3,1,0:T(8,128)(2,1)S(1)} %fusion.69), channel_id=1, source_target_pairs={{0,16},{16,32},{32,48},{48,64},{64,80},{80,96},{96,112},{112,128},... | collective-permute-start | bytes 1376264 | tf_op jit(solution)/shard_map/while/body/eval_jaxpr/ppermute | solution.py:16
  169.6 12.0 %collective-permute-start = (bf16[1,14,128,128]{2,3,1,0:T(8,128)(2,1)S(1)}, bf16[1,14,128,128]{2,3,1,0:T(8,128)(2,1)S(1)}, u32[]{:S(2)}, u32[]{:S(2)}) collective-permute-start(bf16[1,14,128,128]{2,3,1,0:T(8,128)(2,1)S(1)} %fusion.69), channel_id=1, source_target_pairs={{0,16},{16,32},{32,48},{48,64},{64,80},{80,96},{96,112},{112,128},... | collective-permute-start | bytes 1376264 | tf_op jit(solution)/shard_map/while/body/eval_jaxpr/ppermute | solution.py:16
  183.6 13.1 %collective-permute-start = (bf16[1,14,128,128]{2,3,1,0:T(8,128)(2,1)S(1)}, bf16[1,14,128,128]{2,3,1,0:T(8,128)(2,1)S(1)}, u32[]{:S(2)}, u32[]{:S(2)}) collective-permute-start(bf16[1,14,128,128]{2,3,1,0:T(8,128)(2,1)S(1)} %fusion.69), channel_id=1, source_target_pairs={{0,16},{16,32},{32,48},{48,64},{64,80},{80,96},{96,112},{112,128},... | collective-permute-start | bytes 1376264 | tf_op jit(solution)/shard_map/while/body/eval_jaxpr/ppermute | solution.py:16
  198.6 14.2 %collective-permute-start = (bf16[1,14,128,128]{2,3,1,0:T(8,128)(2,1)S(1)}, bf16[1,14,128,128]{2,3,1,0:T(8,128)(2,1)S(1)}, u32[]{:S(2)}, u32[]{:S(2)}) collective-permute-start(bf16[1,14,128,128]{2,3,1,0:T(8,128)(2,1)S(1)} %fusion.69), channel_id=1, source_target_pairs={{0,16},{16,32},{32,48},{48,64},{64,80},{80,96},{96,112},{112,128},... | collective-permute-start | bytes 1376264 | tf_op jit(solution)/shard_map/while/body/eval_jaxpr/ppermute | solution.py:16
  214.8 15.3 %collective-permute-start = (bf16[1,14,128,128]{2,3,1,0:T(8,128)(2,1)S(1)}, bf16[1,14,128,128]{2,3,1,0:T(8,128)(2,1)S(1)}, u32[]{:S(2)}, u32[]{:S(2)}) collective-permute-start(bf16[1,14,128,128]{2,3,1,0:T(8,128)(2,1)S(1)} %fusion.69), channel_id=1, source_target_pairs={{0,16},{16,32},{32,48},{48,64},{64,80},{80,96},{96,112},{112,128},... | collective-permute-start | bytes 1376264 | tf_op jit(solution)/shard_map/while/body/eval_jaxpr/ppermute | solution.py:16
  232.0 16.4 %collective-permute-start = (bf16[1,14,128,128]{2,3,1,0:T(8,128)(2,1)S(1)}, bf16[1,14,128,128]{2,3,1,0:T(8,128)(2,1)S(1)}, u32[]{:S(2)}, u32[]{:S(2)}) collective-permute-start(bf16[1,14,128,128]{2,3,1,0:T(8,128)(2,1)S(1)} %fusion.69), channel_id=1, source_target_pairs={{0,16},{16,32},{32,48},{48,64},{64,80},{80,96},{96,112},{112,128},... | collective-permute-start | bytes 1376264 | tf_op jit(solution)/shard_map/while/body/eval_jaxpr/ppermute | solution.py:16
  255.1 11.0 %copy-start.3 = (f32[14,14]{1,0:T(8,128)S(1)}, f32[14,14]{1,0:T(8,128)}, u32[]{:S(2)}) copy-start(f32[14,14]{1,0:T(8,128)} %convert_element_type.122) | copy-start | bytes 2356
  255.1 11.0 %copy-start.8 = (bf16[14,16,16,14]{2,1,3,0:T(8,128)(2,1)S(1)}, bf16[14,16,16,14]{2,1,3,0:T(8,128)(2,1)}, u32[]{:S(2)}) copy-start(bf16[14,16,16,14]{2,1,3,0:T(8,128)(2,1)} %param.16) | copy-start | bytes 301060
  266.1 11.6 %copy-start.5 = (s32[16]{0:T(128)S(1)}, s32[16]{0:T(128)}, u32[]{:S(2)}) copy-start(s32[16]{0:T(128)} %get-tuple-element.122) | copy-start | bytes 196
  266.1 11.6 %copy-start = (bf16[1,1,16,128,128]{4,3,2,1,0:T(8,128)(2,1)S(1)}, bf16[1,1,16,128,128]{4,3,2,1,0:T(8,128)(2,1)}, u32[]{:S(2)}) copy-start(bf16[1,1,16,128,128]{4,3,2,1,0:T(8,128)(2,1)} %param.15) | copy-start | bytes 1572868
  266.1 12.5 %copy-start.2 = (bf16[1,1,14,128,128]{4,3,2,1,0:T(8,128)(2,1)S(1)}, bf16[1,1,14,128,128]{4,3,2,1,0:T(8,128)(2,1)}, u32[]{:S(2)}) copy-start(bf16[1,1,14,128,128]{4,3,2,1,0:T(8,128)(2,1)} %param.14) | copy-start | bytes 1376260
  375.4 11.4 %copy-start.7 = (pred[16]{0:T(512)(128)(4,1)S(1)}, pred[16]{0:T(512)(128)(4,1)}, u32[]{:S(2)}) copy-start(pred[16]{0:T(512)(128)(4,1)} %get-tuple-element.120) | copy-start | bytes 52
  394.3 51.1 %copy-start.1 = (f32[16,128,128]{2,1,0:T(8,128)}, f32[16,128,128]{2,1,0:T(8,128)S(1)}, u32[]{:S(2)}) copy-start(f32[16,128,128]{2,1,0:T(8,128)S(1)} %get-tuple-element.126) | copy-start | bytes 3145732
  (4 other events, 37.1 us)
where the time goes:
time: 537 us; the launch traced here: 536 us
  waiting for transfers between devices  171 us (32%)
  blocking collectives  161 us (30%)
  matrix products  101 us (19%)
  local copies, waits for them, and re-layouts  42.8 us (8%)
  starting transfers between devices  36 us (7%)
  other arithmetic  15.5 us (3%)
  between operations  7.98 us (1%)
    ppermute x15, waiting for transfers between devices, from_behind(): return lax.ppermute(block, axis, route)  171 us
    psum x3, blocking collectives, body(): lax.psum((jnp.sum(tensor * tensor), jnp.sum(tensor * image)), 'sector')  88.9 us
    psum x3, blocking collectives, body(): new_sq = lax.psum(jnp.sum(updated * updated), 'sector')  72.4 us
    dot_general x3, matrix products, body(): jnp.einsum('qwpxv,qxwad->qpvad', operator, first, preferred_element_type=...  34.3 us
    another operation x3, local copies, waits for them, and re-layouts  32.7 us
    ppermute x15, starting transfers between devices, from_behind(): return lax.ppermute(block, axis, route)  30 us
    dot_general x3, matrix products, body(): jnp.einsum('qpvad,qpvbd->qpab', second, chosen, preferred_element_type=jn...  22.2 us
    dot_general x3, matrix products, body(): jnp.einsum('qwae,qped->qpwad', env_bf, tensor.astype(jnp.bfloat16), prefe...  16.8 us
  transfers between devices with their start and end apart: 17, of which 15 were waited for; matrix products, arithmetic and copies ran while one was open for 13% of the time, Pallas kernels for 0%

commit v1 on v0

v1 whole, which is shorter than its diff:
```python
import functools

import jax
import jax.numpy as jnp
from jax import lax
from jax.experimental import pallas as pl
from jax.experimental.pallas import tpu as pltpu
from jax.sharding import PartitionSpec as P

ITERS = 3
CARRY = 0.8
STEP = 0.5
F32 = jnp.float32
BF16 = jnp.bfloat16
VMEM_LIMIT = 56 * 2**20

SMEM_SPEC = pl.BlockSpec(memory_space=pltpu.SMEM)
VMEM_SPEC = pl.BlockSpec(memory_space=pltpu.VMEM)
ANY_SPEC = pl.BlockSpec(memory_space=pl.ANY)
PARAMS = pltpu.CompilerParams(vmem_limit_bytes=VMEM_LIMIT)

PAIRS = [(i, j) for j in range(ITERS + 1) for i in range(j + 1)]


def pack_kernel(add_ref, transfer_ref, out_ref):
    channels, rows, _ = add_ref.shape
    slots = out_ref.shape[0]
    moved = transfer_ref[...].astype(BF16)
    for w in range(slots):
        if w < channels:
            out_ref[w, :rows, :] = add_ref[w].astype(BF16)
        else:
            out_ref[w, :rows, :] = jnp.zeros((rows, rows), BF16)
        out_ref[w, rows:, :] = moved


def scan_kernel(got_ref, left_ref, right_ref, env_ref, wide_ref, edge, tall, sem):
    segments, _, rows = got_ref.shape
    channels = left_ref.shape[0]
    mine = jnp.minimum(lax.axis_index("chain"), channels - 1)
    fetch = pltpu.make_async_copy(left_ref.at[mine], edge, sem)
    fetch.start()
    slots = tall.shape[0] // rows
    for v in range(slots):
        if v < channels:
            tall[pl.ds(v, rows, stride=slots), :] = right_ref[v].astype(F32).T
        else:
            tall[pl.ds(v, rows, stride=slots), :] = jnp.zeros((rows, rows), F32)
    for n in range(slots):
        wide_ref[:, n * rows : (n + 1) * rows] = tall[n * rows : (n + 1) * rows, :].T.astype(BF16)
    fetch.wait()
    env = edge[...].T
    env_ref[0] = env.astype(BF16)
    for c in range(segments - 1):
        moved = got_ref[c, rows:, :]
        half = CARRY * env + jnp.dot(env.astype(BF16), moved, preferred_element_type=F32)
        env = (
            CARRY * half
            + jnp.dot(moved.T, half.astype(BF16), preferred_element_type=F32)
            + got_ref[c, :rows, :].astype(F32).T
        )
        env_ref[c + 1] = env.astype(BF16)


def slot_limit(q, shift, size_ref):
    sectors = size_ref.shape[0]
    target = q + shift
    valid = jnp.logical_and(target >= 0, target < sectors)
    return jnp.where(valid, size_ref[jnp.clip(target, 0, sectors - 1)], 0)


def ham_kernel(
    shift_ref, size_ref, env_ref, below_ref, own_ref, above_ref, psi_ref, mpo_ref, chan_ref,
    stats_ref, image_ref,
    vecs, unit, left, right, mix, first, second,
):
    q = lax.axis_index("sector")
    channels, states = mpo_ref.shape[:2]
    rows = psi_ref.shape[-1]
    deep = channels * states
    slots = mix.shape[0] // states
    state_of = lax.broadcasted_iota(jnp.int32, (1, deep), 1) % states
    shift_of = jnp.zeros((1, deep), jnp.int32)
    for p2 in range(states):
        shift_of = jnp.where(state_of == p2, shift_ref[0, p2], shift_of)
    spread = (
        lax.broadcasted_iota(jnp.int32, (channels, deep), 1) // states
        == lax.broadcasted_iota(jnp.int32, (channels, deep), 0)
    ).astype(F32)
    kept = lax.dot_general(
        chan_ref[...].astype(F32), spread, (((0,), (0,)), ((), ())), preferred_element_type=F32
    )
    kept = jnp.concatenate([kept, jnp.zeros((slots - channels, deep), F32)], axis=0)
    pick = (
        lax.broadcasted_iota(jnp.int32, (slots, channels), 0)
        == lax.broadcasted_iota(jnp.int32, (slots, channels), 1)
    ).astype(BF16)
    for p in range(states):
        block = jnp.concatenate([mpo_ref[w, p] for w in range(channels)], axis=0)
        turned = lax.dot_general(
            pick, block, (((1,), (1,)), ((), ())), preferred_element_type=F32
        )
        same = (shift_of == shift_ref[0, p]).astype(F32)
        mix[p * slots : (p + 1) * slots, :] = (turned * kept * same).astype(BF16)
    for w in range(channels):
        left[:, w * rows : (w + 1) * rows] = env_ref[w]
    right[0] = below_ref[...]
    right[1] = own_ref[...]
    right[2] = above_ref[...]

    row_id = lax.broadcasted_iota(jnp.int32, (rows, rows), 0)
    col_id = lax.broadcasted_iota(jnp.int32, (rows, rows), 1)
    own_size = size_ref[q]

    def masked(p, block):
        limit = slot_limit(q, shift_ref[0, p], size_ref)
        live = jnp.logical_and(row_id < limit, col_id < own_size)
        return jnp.where(live, block, 0.0)

    def inner(i, j):
        return jnp.sum(
            jnp.sum(vecs[i] * vecs[j], axis=0, keepdims=True), axis=1, keepdims=True
        )

    for p in range(states):
        vecs[0, pl.ds(p, rows, stride=states), :] = masked(p, psi_ref[p].astype(F32).T)
    gram = {(0, 0): inner(0, 0)}
    scales = []
    chunk = first.shape[0]
    for k in range(ITERS):
        size = gram[k, k]
        scale = jnp.where(size > 1e-30, lax.rsqrt(jnp.maximum(size, 1e-30)), 1.0)
        scales.append(scale)
        unit[...] = (vecs[k] * scale).astype(BF16)

        def columns(i, carry):
            start = pl.multiple_of(i * chunk * states, chunk * states)
            part = unit[pl.ds(start, chunk * states), :]
            for n in range(0, channels, 2):
                y = jnp.dot(
                    part, left[:, n * rows : (n + 2) * rows], preferred_element_type=F32
                ).astype(BF16)
                for d in range(chunk):
                    for h in range(2):
                        first[d, (n + h) * states : (n + h + 1) * states, :] = y[
                            d * states : (d + 1) * states, h * rows : (h + 1) * rows
                        ]
            for d in range(0, chunk, 2):
                pair = jnp.concatenate([first[d], first[d + 1]], axis=1)
                z = jnp.dot(mix[...], pair, preferred_element_type=F32).astype(BF16)
                for h in range(2):
                    place = pl.ds(pl.multiple_of((i * chunk + d + h) * slots, slots), slots)
                    for p in range(states):
                        second[p, place, :] = z[
                            p * slots : (p + 1) * slots, h * rows : (h + 1) * rows
                        ]
            return carry

        lax.fori_loop(0, rows // chunk, columns, 0)
        for p in range(states):
            block = jnp.dot(
                right[shift_ref[0, p] + 1], second[p], preferred_element_type=F32
            )
            block = masked(p, block)
            vecs[k + 1, pl.ds(p, rows, stride=states), :] = block
            image_ref[k, p] = block.T
        for j in range(k + 2):
            gram[j, k + 1] = inner(j, k + 1)
    entries = [jnp.broadcast_to(gram[pair], (1, rows)) for pair in PAIRS]
    entries += [jnp.broadcast_to(scale, (1, rows)) for scale in scales]
    entries.append(jnp.zeros((stats_ref.shape[1] - len(entries), rows), F32))
    stats = jnp.concatenate(entries, axis=0)
    for s in range(stats_ref.shape[0]):
        stats_ref[s] = stats


def final_kernel(shift_ref, size_ref, stats_ref, psi_ref, image_ref, out_ref, energy_ref):
    q = lax.axis_index("sector")
    sectors, _, rows = stats_ref.shape
    states = psi_ref.shape[0]
    gram = {}
    for n, (i, j) in enumerate(PAIRS):
        gram[i, j] = gram[j, i] = stats_ref[:, n, :]
    scales = [stats_ref[:, len(PAIRS) + j, :] for j in range(ITERS)]

    def product(a, b):
        total = None
        for i, x in enumerate(a):
            for j, y in enumerate(b):
                if x is not None and y is not None:
                    term = x * y * gram[i, j]
                    total = term if total is None else total + term
        return jnp.sum(total, axis=0, keepdims=True)

    coefs = [jnp.ones((sectors, rows), F32)]
    rayleigh = None
    for _ in range(ITERS):
        image = [None] + [c / s for c, s in zip(coefs, scales)]
        rayleigh = product(coefs, image) / product(coefs, coefs)
        updated = []
        for j in range(len(coefs) + 1):
            value = 0.0
            if j < len(coefs):
                value = (1.0 + STEP * rayleigh) * coefs[j]
            if image[j] is not None:
                value = value - STEP * image[j]
            updated.append(value)
        norm = lax.rsqrt(product(updated, updated))
        coefs = [c * norm for c in updated]
    energy_ref[0] = rayleigh[0, 0]
    sector_id = lax.broadcasted_iota(jnp.int32, (sectors, rows), 0)
    own = [jnp.sum(jnp.where(sector_id == q, c, 0.0), axis=0, keepdims=True) for c in coefs]
    row_id = lax.broadcasted_iota(jnp.int32, (rows, rows), 0)
    col_id = lax.broadcasted_iota(jnp.int32, (rows, rows), 1)
    own_size = size_ref[q]
    for p in range(states):
        limit = slot_limit(q, shift_ref[0, p], size_ref)
        live = jnp.logical_and(col_id < limit, row_id < own_size)
        total = own[0] * jnp.where(live, psi_ref[p].astype(F32), 0.0)
        for k in range(ITERS):
            total = total + own[k + 1] * image_ref[k, p]
        out_ref[p] = total.astype(BF16)


def body(
    left_edge, transfer, completed, right_env, psi_init, mpo, mpo_mask, charge_shift, block_size
):
    channels, rows = left_edge.shape[1:3]
    segments, sectors = lax.axis_size("chain"), lax.axis_size("sector")
    states = psi_init.shape[2]
    slots = 16
    payload = pl.pallas_call(
        pack_kernel,
        out_shape=jax.ShapeDtypeStruct((segments, 2 * rows, rows), BF16),
        in_specs=[VMEM_SPEC] * 2,
        out_specs=VMEM_SPEC,
        compiler_params=PARAMS,
    )(completed[0, 0], transfer[0, 0])
    got = lax.all_to_all(payload, "chain", 0, 0, tiled=True)
    env_out, wide = pl.pallas_call(
        scan_kernel,
        out_shape=(
            jax.ShapeDtypeStruct((segments, rows, rows), BF16),
            jax.ShapeDtypeStruct((rows, rows * slots), BF16),
        ),
        in_specs=[VMEM_SPEC, ANY_SPEC, VMEM_SPEC],
        out_specs=(VMEM_SPEC, VMEM_SPEC),
        scratch_shapes=[
            pltpu.VMEM((rows, rows), F32),
            pltpu.VMEM((rows * slots, rows), F32),
            pltpu.SemaphoreType.DMA,
        ],
        compiler_params=PARAMS,
    )(got, left_edge[0], right_env[0, 0])
    below = lax.ppermute(wide, "sector", [(i, i + 1) for i in range(sectors - 1)])
    above = lax.ppermute(wide, "sector", [(i + 1, i) for i in range(sectors - 1)])
    env = lax.all_to_all(env_out, "chain", 0, 0, tiled=True)
    chunk = 16
    stats, image = pl.pallas_call(
        ham_kernel,
        out_shape=(
            jax.ShapeDtypeStruct((sectors, 16, rows), F32),
            jax.ShapeDtypeStruct((ITERS, states, rows, rows), F32),
        ),
        in_specs=[SMEM_SPEC] * 2 + [VMEM_SPEC] * 7,
        out_specs=(VMEM_SPEC, VMEM_SPEC),
        scratch_shapes=[
            pltpu.VMEM((ITERS + 1, rows * states, rows), F32),
            pltpu.VMEM((rows * states, rows), BF16),
            pltpu.VMEM((rows, channels * rows), BF16),
            pltpu.VMEM((3, rows, rows * slots), BF16),
            pltpu.VMEM((states * slots, channels * states), BF16),
            pltpu.VMEM((chunk, channels * states, rows), BF16),
            pltpu.VMEM((states, rows * slots, rows), BF16),
        ],
        compiler_params=PARAMS,
    )(charge_shift, block_size, env, below, wide, above, psi_init[0, 0], mpo, mpo_mask)
    stats = lax.all_to_all(stats, "sector", 0, 0, tiled=True)
    out, energy = pl.pallas_call(
        final_kernel,
        out_shape=(
            jax.ShapeDtypeStruct((states, rows, rows), BF16),
            jax.ShapeDtypeStruct((1,), F32),
        ),
        in_specs=[SMEM_SPEC] * 2 + [VMEM_SPEC] * 3,
        out_specs=(VMEM_SPEC, SMEM_SPEC),
        compiler_params=PARAMS,
    )(charge_shift, block_size, stats, psi_init[0, 0], image)
    return out[None, None], energy


def solution(mesh):
    placed = (
        P("sector", None, None, None),
        P("chain", "sector", None, None),
        P("chain", "sector", None, None, None),
        P("chain", "sector", None, None, None),
        P("chain", "sector", None, None, None),
        P(),
        P(),
        P("sector", None),
        P(),
    )
    return jax.shard_map(
        body,
        mesh=mesh,
        in_specs=placed,
        out_specs=(P("chain", "sector", None, None, None), P("chain")),
        check_vma=False,
    )
```

time: 537 us -> 112 us (0.21)
  the two profiles are of different devices: /device:TPU:25 before, /device:TPU:1 now
where the time goes in v1:
time: 112 us; the launch traced here: 111 us
  Pallas kernels  45.2 us (40%)
  blocking collectives  42 us (38%)
  starting transfers between devices  10.9 us (10%)
  waiting for transfers between devices  8.89 us (8%)
  local copies, waits for them, and re-layouts  3.48 us (3%)
    pallas_call x1, Pallas kernels, body(): pl.pallas_call(ham_kernel, out_shape=(jax.ShapeDtypeStruct((sectors, 16,...  32.5 us
    all_to_all x1, blocking collectives, body(): got = lax.all_to_all(payload, 'chain', 0, 0, tiled=True)  23.9 us
    all_to_all x1, blocking collectives, body(): stats = lax.all_to_all(stats, 'sector', 0, 0, tiled=True)  18.1 us
    all_to_all x1, waiting for transfers between devices, body(): env = lax.all_to_all(env_out, 'chain', 0, 0, tiled=True)  8.88 us
    pallas_call x1, Pallas kernels, body(): pl.pallas_call(scan_kernel, out_shape=(jax.ShapeDtypeStruct((segments, ro...  6.87 us
    ppermute x1, starting transfers between devices, body(): lax.ppermute(wide, 'sector', [(i + 1, i) for i in range(sectors - 1)])  3.89 us
    all_to_all x1, starting transfers between devices, body(): env = lax.all_to_all(env_out, 'chain', 0, 0, tiled=True)  3.59 us
    unnamed x9, local copies, waits for them, and re-layouts  3.48 us
  transfers between devices with their start and end apart: 3, of which 1 were waited for; matrix products, arithmetic and copies ran while one was open for 2% of the time, Pallas kernels for 0%

profile of v1, /device:TPU:1, one launch (start us, length us, event | category | flops | bytes accessed | tf_op | source)
XLA Modules:
  0.0 111.1 jit_solution(15611431449411642127)
XLA Ops:
  0.6 2.3 %shard_map.104 = bf16[16,256,128]{2,1,0:T(8,128)(2,1)} custom-call(f32[14,128,128]{2,1,0:T(8,128)} %bitcast.8, f32[128,128]{1,0:T(8,128)} %bitcast.11), custom_call_target="tpu_custom_call" | custom-call | tf_op jit(solution)/shard_map/pallas_call | solution.py:232
  2.9 0.0 copy-start.1
  2.9 23.9 %all_to_all.15.got_ref = bf16[16,256,128]{2,1,0:T(8,128)(2,1)} all-to-all(bf16[16,256,128]{2,1,0:T(8,128)(2,1)} %shard_map.104), channel_id=1, replica_groups=mesh['chain'=16,'sector'=16] {'chain'}, dimensions={0} | all-to-all | bytes 2097152 | tf_op jit(solution)/shard_map/all_to_all | solution.py:239
  26.9 6.9 %shard_map.105 = (bf16[16,128,128]{2,1,0:T(8,128)(2,1)}, bf16[128,2048]{1,0:T(8,128)(2,1)}) custom-call(bf16[16,256,128]{2,1,0:T(8,128)(2,1)} %all_to_all.15.got_ref, f32[14,128,128]{2,1,0:T(8,128)} %bitcast.9, bf16[14,128,128]{2,1,0:T(8,128)(2,1)} %bitcast.10), custom_call_target="tpu_custom_call" | custom-call | tf_op jit(solution)/shard_map/pallas_call | solution.py:240
  33.8 3.9 %collective-permute-start.1 = (bf16[128,2048]{1,0:T(8,128)(2,1)}, bf16[128,2048]{1,0:T(8,128)(2,1)S(1)}, u32[]{:S(2)}, u32[]{:S(2)}) collective-permute-start(bf16[128,2048]{1,0:T(8,128)(2,1)} %get-tuple-element.9.own_ref), channel_id=1, source_target_pairs={{1,0},{2,1},{3,2},{4,3},{5,4},{6,5},{7,6},{8,7},{9,8},{10,9},{11,1... | collective-permute-start | bytes 1572872 | tf_op jit(solution)/shard_map/ppermute | solution.py:256
  37.6 3.4 %collective-permute-start = (bf16[128,2048]{1,0:T(8,128)(2,1)}, bf16[128,2048]{1,0:T(8,128)(2,1)S(1)}, u32[]{:S(2)}, u32[]{:S(2)}) collective-permute-start(bf16[128,2048]{1,0:T(8,128)(2,1)} %get-tuple-element.9.own_ref), channel_id=1, source_target_pairs={{0,1},{1,2},{2,3},{3,4},{4,5},{5,6},{6,7},{7,8},{8,9},{9,10},{10,1... | collective-permute-start | bytes 1572872 | tf_op jit(solution)/shard_map/ppermute | solution.py:255
  41.1 3.6 %all-to-all-start.1 = ((bf16[16,128,128]{2,1,0:T(8,128)(2,1)}), bf16[16,128,128]{2,1,0:T(8,128)(2,1)S(1)}, u32[]{:S(2)}, u32[]{:S(2)}) async-start(bf16[16,128,128]{2,1,0:T(8,128)(2,1)} %get-tuple-element.8), calls=%async_computation.1 | async-start | bytes 1048576 | tf_op jit(solution)/shard_map/all_to_all | solution.py:257
  44.7 0.0 copy-done.1
  44.7 2.3 %copy.11.mpo_ref = bf16[14,16,16,14]{3,2,1,0:T(8,128)(2,1)} copy(bf16[14,16,16,14]{2,1,3,0:T(8,128)(2,1)S(1)} %copy-done.1) | data formatting | bytes 200704 | tf_op args[5]
  47.0 8.9 %all-to-all-done.1.env_ref = bf16[16,128,128]{2,1,0:T(8,128)(2,1)S(1)} async-done(((bf16[16,128,128]{2,1,0:T(8,128)(2,1)}), bf16[16,128,128]{2,1,0:T(8,128)(2,1)S(1)}, u32[]{:S(2)}, u32[]{:S(2)}) %all-to-all-start.1) | async-done | bytes 524320 | tf_op jit(solution)/shard_map/all_to_all | solution.py:257
  55.9 0.0 copy-start
  55.9 0.0 collective-permute-done.1.above_ref
  55.9 0.0 copy-start.2
  55.9 0.0 collective-permute-done.below_ref
  55.9 0.0 copy-start.3
  55.9 0.8 copy-done
  56.7 0.2 copy-done.2
  56.9 0.2 copy-done.3
  57.1 32.5 %shard_map.106 = (f32[16,16,128]{2,1,0:T(8,128)}, f32[3,16,128,128]{3,2,1,0:T(8,128)}) custom-call(s32[1,16]{1,0:T(1,128)} %shift_ref.3, s32[16]{0:T(128)} %size_ref.3, bf16[16,128,128]{2,1,0:T(8,128)(2,1)} %copy-done, bf16[128,2048]{1,0:T(8,128)(2,1)} %copy-done.3, bf16[128,2048]{1,0:T(8,128)(2,1)} %get-tuple-element.9.own_ref, ...), custom_call_target="tpu_custom_call" | custom-call | tf_op jit(solution)/shard_map/pallas_call | solution.py:259
  89.6 18.1 %all_to_all.16.stats_ref = f32[16,16,128]{2,1,0:T(8,128)} all-to-all(f32[16,16,128]{2,1,0:T(8,128)} %get-tuple-element.10), channel_id=1, replica_groups=mesh['chain'=16,'sector'=16] {'sector'}, dimensions={0} | all-to-all | bytes 262144 | tf_op jit(solution)/shard_map/all_to_all | solution.py:278
  107.7 3.5 %shard_map.107 = (bf16[16,128,128]{2,1,0:T(8,128)(2,1)}, f32[1]{0:T(128)}) custom-call(s32[1,16]{1,0:T(1,128)} %shift_ref.3, s32[16]{0:T(128)} %size_ref.3, f32[16,16,128]{2,1,0:T(8,128)} %all_to_all.16.stats_ref, bf16[16,128,128]{2,1,0:T(8,128)(2,1)} %bitcast.7, f32[3,16,128,128]{3,2,1,0:T(8,128)} %get-tuple-element.11.image_ref), custom_call_target="tpu_custom_call" | custom-call | tf_op jit(solution)/shard_map/pallas_call | solution.py:279
Async XLA Ops:
  2.9 41.8 %copy-start.1 = (bf16[14,16,16,14]{2,1,3,0:T(8,128)(2,1)S(1)}, bf16[14,16,16,14]{2,1,3,0:T(8,128)(2,1)}, u32[]{:S(2)}) copy-start(bf16[14,16,16,14]{2,1,3,0:T(8,128)(2,1)} %param.14) | copy-start | bytes 301060
  33.8 22.2 %collective-permute-start.1 = (bf16[128,2048]{1,0:T(8,128)(2,1)}, bf16[128,2048]{1,0:T(8,128)(2,1)S(1)}, u32[]{:S(2)}, u32[]{:S(2)}) collective-permute-start(bf16[128,2048]{1,0:T(8,128)(2,1)} %get-tuple-element.9.own_ref), channel_id=1, source_target_pairs={{1,0},{2,1},{3,2},{4,3},{5,4},{6,5},{7,6},{8,7},{9,8},{10,9},{11,1... | collective-permute-start | bytes 1572872 | tf_op jit(solution)/shard_map/ppermute | solution.py:256
  37.6 18.3 %collective-permute-start = (bf16[128,2048]{1,0:T(8,128)(2,1)}, bf16[128,2048]{1,0:T(8,128)(2,1)S(1)}, u32[]{:S(2)}, u32[]{:S(2)}) collective-permute-start(bf16[128,2048]{1,0:T(8,128)(2,1)} %get-tuple-element.9.own_ref), channel_id=1, source_target_pairs={{0,1},{1,2},{2,3},{3,4},{4,5},{5,6},{6,7},{7,8},{8,9},{9,10},{10,1... | collective-permute-start | bytes 1572872 | tf_op jit(solution)/shard_map/ppermute | solution.py:255
  41.1 14.8 %all-to-all-start.1 = ((bf16[16,128,128]{2,1,0:T(8,128)(2,1)}), bf16[16,128,128]{2,1,0:T(8,128)(2,1)S(1)}, u32[]{:S(2)}, u32[]{:S(2)}) async-start(bf16[16,128,128]{2,1,0:T(8,128)(2,1)} %get-tuple-element.8), calls=%async_computation.1 | async-start | bytes 1048576 | tf_op jit(solution)/shard_map/all_to_all | solution.py:257
  55.9 0.8 copy-start
  55.9 1.0 copy-start.2
  55.9 1.2 %copy-start.3 = (bf16[128,2048]{1,0:T(8,128)(2,1)}, bf16[128,2048]{1,0:T(8,128)(2,1)S(1)}, u32[]{:S(2)}) copy-start(bf16[128,2048]{1,0:T(8,128)(2,1)S(1)} %collective-permute-done.below_ref) | copy-start | bytes 1572868

commit v2 on v1

v2 whole, which is shorter than its diff:
```python
import functools

import jax
import jax.numpy as jnp
from jax import lax
from jax.experimental import pallas as pl
from jax.experimental.pallas import tpu as pltpu
from jax.sharding import PartitionSpec as P

ITERS = 3
CARRY = 0.8
STEP = 0.5
F32 = jnp.float32
BF16 = jnp.bfloat16
VMEM_LIMIT = 63 * 2**20

SMEM_SPEC = pl.BlockSpec(memory_space=pltpu.SMEM)
VMEM_SPEC = pl.BlockSpec(memory_space=pltpu.VMEM)
HBM_SPEC = pl.BlockSpec(memory_space=pltpu.HBM)

PAIRS = [(i, j) for j in range(ITERS + 1) for i in range(j + 1)]


def pack_kernel(add_ref, transfer_ref, out_ref, adds, moved, block, in_sems, out_sems):
    channels, rows, _ = add_ref.shape
    slots, group = out_ref.shape[0], channels // 7
    fetch = pltpu.make_async_copy(transfer_ref, moved, in_sems.at[7])
    fetch.start()
    fetches, stores = [], []
    for n in range(7):
        part = pl.ds(n * group, group)
        fetches.append(pltpu.make_async_copy(add_ref.at[part], adds.at[part], in_sems.at[n]))
        fetches[n].start()
    fetch.wait()
    for w in range(slots):
        block[w, rows:, :] = moved[...].astype(BF16)
    for w in range(channels, slots):
        block[w, :rows, :] = jnp.zeros((rows, rows), BF16)
    part = pl.ds(channels, slots - channels)
    stores.append(pltpu.make_async_copy(block.at[part], out_ref.at[part], out_sems.at[7]))
    stores[0].start()
    for n in range(7):
        fetches[n].wait()
        for w in range(n * group, (n + 1) * group):
            block[w, :rows, :] = adds[w].astype(BF16)
        part = pl.ds(n * group, group)
        stores.append(pltpu.make_async_copy(block.at[part], out_ref.at[part], out_sems.at[n]))
        stores[-1].start()
    for store in stores:
        store.wait()


def congruence(env, scale, rest, add):
    rest = rest.astype(BF16)
    half = scale * env + jnp.dot(env.astype(BF16), rest, preferred_element_type=F32)
    moved = scale * half + jnp.dot(rest.T, half.astype(BF16), preferred_element_type=F32)
    return moved + add


def scan_kernel(got_hbm, left_hbm, env_ref, edge, got_ref, sem, got_sems):
    segments, _, rows = got_ref.shape
    channels = left_hbm.shape[0]
    mine = jnp.minimum(lax.axis_index("chain"), channels - 1)
    fetch = pltpu.make_async_copy(left_hbm.at[mine], edge, sem)
    fetch.start()
    width = 4
    groups = segments // width
    fetches = []
    for n in range(groups):
        part = pl.ds(n * width, width)
        fetches.append(pltpu.make_async_copy(got_hbm.at[part], got_ref.at[part], got_sems.at[n]))
        fetches[n].start()
    fetch.wait()
    for n in range(groups):
        fetches[n].wait()

    def step(c):
        return got_ref[c, rows:, :], got_ref[c, :rows, :].astype(F32)

    current = [edge[...]] + [None] * (groups - 1)
    begun = [[] for _ in range(groups)]
    factors = [[] for _ in range(groups)]
    env_ref[0] = edge[...].astype(BF16)
    for j in range(width):
        for g in range(groups):
            c = g * width + j
            if c == segments - 1:
                continue
            rest, add = step(c)
            if g == 0:
                current[0] = congruence(current[0], CARRY, rest, add)
                env_ref[c + 1] = current[0].astype(BF16)
            elif j == 0:
                begun[g].append(add)
                factors[g].append((CARRY, rest))
            else:
                begun[g].append(congruence(begun[g][-1], CARRY, rest, add))
                scale, other = factors[g][-1]
                product = (
                    CARRY * other.astype(F32)
                    + scale * rest.astype(F32)
                    + jnp.dot(other.astype(BF16), rest, preferred_element_type=F32)
                )
                factors[g].append((scale * CARRY, product))
    env = current[0]
    for g in range(1, groups):
        first = env
        for j in reversed(range(len(begun[g]))):
            block = congruence(first, *factors[g][j], begun[g][j])
            env_ref[g * width + j + 1] = block.astype(BF16)
            if j == width - 1:
                env = block


def slot_limit(q, shift, size_ref):
    sectors = size_ref.shape[0]
    target = q + shift
    valid = jnp.logical_and(target >= 0, target < sectors)
    return jnp.where(valid, size_ref[jnp.clip(target, 0, sectors - 1)], 0)


def fill_operator(mix, shift_ref, mpo_ref, chan_ref, slots, by_v):
    channels, _, states, _ = mpo_ref.shape
    deep = channels * states

    def ids(shape, dim):
        return lax.broadcasted_iota(jnp.int32, shape, dim)

    total = jnp.zeros((deep, deep), F32)
    for c in range(channels):
        tiles = [mpo_ref[c, o] if by_v else mpo_ref[o, c] for o in range(channels)]
        place = (ids((states, deep), 1) == ids((states, deep), 0) + c * states).astype(BF16)
        total = total + jnp.dot(
            jnp.concatenate(tiles, axis=0), place, preferred_element_type=F32
        )
    row, col = ids((states * slots, deep), 0), ids((states * slots, deep), 1)
    order = (col == (row % slots) * states + row // slots).astype(BF16)
    total = jnp.dot(order, total.astype(BF16), preferred_element_type=F32)
    spread = (ids((channels, deep), 1) // states == ids((channels, deep), 0)).astype(F32)
    kept = lax.dot_general(
        chan_ref[...].astype(F32), spread, (((0 if by_v else 1,), (0,)), ((), ())),
        preferred_element_type=F32,
    )
    kept = jnp.concatenate([kept, jnp.zeros((slots - channels, deep), F32)], axis=0)
    state_of = ids((1, deep), 1) % states
    shift_of = jnp.zeros((1, deep), jnp.int32)
    for p in range(states):
        shift_of = jnp.where(state_of == p, shift_ref[0, p], shift_of)
    for p in range(states):
        same = (shift_of == shift_ref[0, p]).astype(F32)
        part = slice(p * slots, (p + 1) * slots)
        mix[part, :] = (total[part, :] * kept * same).astype(BF16)


def pair_up(shift_ref, pair_ref, open_ref):
    states = shift_ref.shape[1]
    for s in range(3):
        open_ref[s] = -1
    count = jnp.int32(0)
    for p in range(states):
        s = shift_ref[0, p] + 1
        waiting = open_ref[s]
        ready = waiting >= 0
        pair_ref[0, count] = jnp.where(ready, waiting, p)
        pair_ref[1, count] = p
        count = count + ready.astype(jnp.int32)
        open_ref[s] = jnp.where(ready, -1, p)
    for s in range(3):
        waiting = open_ref[s]
        pair_ref[0, count] = jnp.maximum(waiting, 0)
        pair_ref[1, count] = jnp.maximum(waiting, 0)
        count = count + (waiting >= 0).astype(jnp.int32)
    pair_ref[2, 0] = count


def block_mask(shift_ref, size_ref, rows, turned):
    q = lax.axis_index("sector")
    row_id = lax.broadcasted_iota(jnp.int32, (rows, rows), 0)
    col_id = lax.broadcasted_iota(jnp.int32, (rows, rows), 1)
    left_id, right_id = (col_id, row_id) if turned else (row_id, col_id)
    own_size = size_ref[q]

    def live(p):
        limit = slot_limit(q, shift_ref[0, p], size_ref)
        return jnp.logical_and(right_id < limit, left_id < own_size)

    return live


def prepare_kernel(
    shift_ref, size_ref, below_ref, own_ref, above_ref, psi_ref, mpo_ref, chan_ref,
    wide_ref, mix_ref, start_ref, pair_ref,
    tall, flat, open_ref,
):
    channels, rows, _ = own_ref.shape
    states = psi_ref.shape[0]
    slots = wide_ref.shape[2] // rows
    pair_up(shift_ref, pair_ref, open_ref)
    fill_operator(mix_ref, shift_ref, mpo_ref, chan_ref, slots, True)
    live = block_mask(shift_ref, size_ref, rows, False)
    for p in range(states):
        block = jnp.where(live(p), psi_ref[p].astype(F32), 0.0)
        flat[pl.ds(p, rows, stride=states), :] = block.T
    start_ref[...] = flat[...].astype(BF16)
    for s, source in enumerate((below_ref, own_ref, above_ref)):
        for v in range(slots):
            place = pl.ds(v, rows, stride=slots)
            if v < channels:
                tall[s, place, :] = source[v].astype(F32).T
            else:
                tall[s, place, :] = jnp.zeros((rows, rows), F32)
        for n in range(slots):
            wide_ref[s, :, n * rows : (n + 1) * rows] = tall[
                s, n * rows : (n + 1) * rows, :
            ].T.astype(BF16)


def ham_kernel(
    shift_ref, size_ref, pair_ref, env_ref, mix_ref, start_ref, psi_hbm, right_hbm,
    stats_ref, image_hbm,
    sums, vecs, unit, left, first, second, psi_ref, right_ref, image_ref, in_sems, image_sems,
):
    states, rows, _ = psi_ref.shape
    channels = mix_ref.shape[1] // states
    slots = mix_ref.shape[0] // states
    pairs = states // 2
    fetches = [
        pltpu.make_async_copy(psi_hbm, psi_ref, in_sems.at[0]),
        pltpu.make_async_copy(right_hbm, right_ref, in_sems.at[1]),
    ]
    for fetch in fetches:
        fetch.start()
    stores = []
    for w in range(channels):
        left[:, w * rows : (w + 1) * rows] = env_ref[w].T
    live = block_mask(shift_ref, size_ref, rows, True)

    def total(x):
        return jnp.sum(jnp.sum(x, axis=0, keepdims=True), axis=1, keepdims=True)

    begin = start_ref[...].astype(F32)
    gram = {(0, 0): total(begin * begin)}
    scales = [jnp.ones((1, 1), F32)]
    chunk = first.shape[0]
    for k in range(ITERS):
        if k:
            size = gram[k, k]
            scale = jnp.where(size > 1e-30, lax.rsqrt(jnp.maximum(size, 1e-30)), 1.0)
            scales.append(scale)
            unit[...] = (vecs[...] * scale).astype(BF16)
        source = unit if k else start_ref

        def columns(i, carry):
            start = pl.multiple_of(i * chunk * states, chunk * states)
            part = source[pl.ds(start, chunk * states), :]
            for n in range(0, channels, 2):
                y = jnp.dot(
                    part, left[:, n * rows : (n + 2) * rows], preferred_element_type=F32
                ).astype(BF16)
                for d in range(chunk):
                    for h in range(2):
                        first[d, (n + h) * states : (n + h + 1) * states, :] = y[
                            d * states : (d + 1) * states, h * rows : (h + 1) * rows
                        ]
            for d in range(0, chunk, 2):
                pair = jnp.concatenate([first[d], first[d + 1]], axis=1)
                z = jnp.dot(mix_ref[...], pair, preferred_element_type=F32).astype(BF16)
                for h in range(2):
                    place = pl.ds(pl.multiple_of((i * chunk + d + h) * slots, slots), slots)
                    for p in range(states):
                        second[p, place, :] = z[
                            p * slots : (p + 1) * slots, h * rows : (h + 1) * rows
                        ]
            return carry

        lax.fori_loop(0, rows // chunk, columns, 0)
        if k == 0:
            for fetch in fetches:
                fetch.wait()
        sums[...] = jnp.zeros(sums.shape, F32)

        def contract(n):
            members = [pair_ref[0, n], pair_ref[1, n]]
            both = jnp.concatenate([second[p] for p in members], axis=1)
            block = jnp.dot(
                right_ref[shift_ref[0, members[0]] + 1], both, preferred_element_type=F32
            )
            counts = [1.0, jnp.where(members[0] == members[1], 0.0, 1.0)]
            for h, p in enumerate(members):
                image = jnp.where(live(p), block[:, h * rows : (h + 1) * rows], 0.0)
                if k + 1 < ITERS:
                    vecs[pl.ds(p, rows, stride=states), :] = image
                image = image.T
                image_ref[k, p] = image.astype(BF16)
                for j in range(k + 2):
                    other = psi_ref[p] if j == 0 else image_ref[min(j, k) - 1, p]
                    other = image if j == k + 1 else other.astype(F32)
                    partial = jnp.sum((image * other).reshape(rows // 8, 8, rows), axis=0)
                    sums[j] += partial * counts[h]

        for n in range(pairs):
            contract(n)

        @pl.when(pair_ref[2, 0] > pairs)
        def _():
            contract(pairs)

        stores.append(pltpu.make_async_copy(image_ref.at[k], image_hbm.at[k], image_sems.at[k]))
        stores[k].start()
        for j in range(k + 2):
            gram[j, k + 1] = total(sums[j])
    entries = [jnp.broadcast_to(gram[pair], (1, rows)) for pair in PAIRS]
    entries += [jnp.broadcast_to(scale, (1, rows)) for scale in scales]
    entries.append(jnp.zeros((stats_ref.shape[1] - len(entries), rows), F32))
    stats = jnp.concatenate(entries, axis=0)
    for s in range(stats_ref.shape[0]):
        stats_ref[s] = stats
    for store in stores:
        store.wait()


def final_kernel(
    shift_ref, size_ref, stats_hbm, psi_hbm, image_hbm, out_hbm, energy_ref,
    stats_ref, psi_ref, image_ref, out_ref, stats_sem, in_sems, out_sems,
):
    stats_fetch = pltpu.make_async_copy(stats_hbm, stats_ref, stats_sem)
    stats_fetch.start()
    groups = in_sems.shape[0]
    fetches, stores = [], []
    for n in range(groups):
        part = pl.ds(n * psi_ref.shape[0] // groups, psi_ref.shape[0] // groups)
        fetches.append(
            pltpu.make_async_copy(image_hbm.at[:, part], image_ref.at[:, part], in_sems.at[n, 0])
        )
        fetches.append(pltpu.make_async_copy(psi_hbm.at[part], psi_ref.at[part], in_sems.at[n, 1]))
        stores.append(pltpu.make_async_copy(out_ref.at[part], out_hbm.at[part], out_sems.at[n]))
    for fetch in fetches:
        fetch.start()
    stats_fetch.wait()
    q = lax.axis_index("sector")
    sectors, _, rows = stats_ref.shape
    states = psi_ref.shape[0]
    gram = {}
    for n, (i, j) in enumerate(PAIRS):
        gram[i, j] = gram[j, i] = stats_ref[:, n, :]
    scales = [stats_ref[:, len(PAIRS) + j, :] for j in range(ITERS)]

    def product(a, b):
        total = None
        for i, x in enumerate(a):
            for j, y in enumerate(b):
                if x is not None and y is not None:
                    term = x * y * gram[i, j]
                    total = term if total is None else total + term
        return jnp.sum(total, axis=0, keepdims=True)

    coefs = [jnp.ones((sectors, rows), F32)]
    rayleigh = None
    for _ in range(ITERS):
        image = [None] + [c / s for c, s in zip(coefs, scales)]
        rayleigh = product(coefs, image) / product(coefs, coefs)
        updated = []
        for j in range(len(coefs) + 1):
            value = 0.0
            if j < len(coefs):
                value = (1.0 + STEP * rayleigh) * coefs[j]
            if image[j] is not None:
                value = value - STEP * image[j]
            updated.append(value)
        norm = lax.rsqrt(product(updated, updated))
        coefs = [c * norm for c in updated]
    energy_ref[0] = rayleigh[0, 0]
    sector_id = lax.broadcasted_iota(jnp.int32, (sectors, rows), 0)
    own = [jnp.sum(jnp.where(sector_id == q, c, 0.0), axis=0, keepdims=True) for c in coefs]
    row_id = lax.broadcasted_iota(jnp.int32, (rows, rows), 0)
    col_id = lax.broadcasted_iota(jnp.int32, (rows, rows), 1)
    own_size = size_ref[q]
    for p in range(states):
        if p % (states // groups) == 0:
            fetches[2 * (p * groups // states)].wait()
            fetches[2 * (p * groups // states) + 1].wait()
        limit = slot_limit(q, shift_ref[0, p], size_ref)
        live = jnp.logical_and(col_id < limit, row_id < own_size)
        total = own[0] * jnp.where(live, psi_ref[p].astype(F32), 0.0)
        for k in range(ITERS):
            total = total + own[k + 1] * image_ref[k, p].astype(F32)
        out_ref[p] = total.astype(BF16)
        if (p + 1) % (states // groups) == 0:
            stores[p * groups // states].start()
    for store in stores:
        store.wait()


def body(
    left_edge, transfer, completed, right_env, psi_init, mpo, mpo_mask, charge_shift, block_size
):
    channels, rows = left_edge.shape[1:3]
    segments, sectors = lax.axis_size("chain"), lax.axis_size("sector")
    states = psi_init.shape[2]
    slots = 16
    deep = channels * states
    own, psi = right_env[0, 0], psi_init[0, 0]
    operator = jnp.transpose(mpo, (0, 3, 1, 2))

    def kernel(function, out_shape, in_specs, scratch, out_specs=None, flops=0, grid=()):
        shapes = out_shape if isinstance(out_shape, tuple) else (out_shape,)
        specs = out_specs or tuple(VMEM_SPEC for _ in shapes)
        return pl.pallas_call(
            function,
            grid=grid,
            out_shape=out_shape,
            in_specs=in_specs,
            out_specs=specs if isinstance(out_shape, tuple) else specs[0],
            scratch_shapes=scratch,
            compiler_params=pltpu.CompilerParams(vmem_limit_bytes=VMEM_LIMIT),
            cost_estimate=pl.CostEstimate(
                flops=flops, bytes_accessed=4 * 2**20, transcendentals=0
            ),
        )

    def shape(*dims, dtype=BF16):
        return jax.ShapeDtypeStruct(dims, dtype)

    payload = kernel(
        pack_kernel,
        shape(segments, 2 * rows, rows),
        [HBM_SPEC] * 2,
        [
            pltpu.VMEM((channels, rows, rows), F32),
            pltpu.VMEM((rows, rows), F32),
            pltpu.VMEM((segments, 2 * rows, rows), BF16),
            pltpu.SemaphoreType.DMA((8,)),
            pltpu.SemaphoreType.DMA((8,)),
        ],
        out_specs=(HBM_SPEC,),
        flops=10**6,
    )(completed[0, 0], transfer[0, 0])
    below = lax.ppermute(own, "sector", [(i, i + 1) for i in range(sectors - 1)])
    above = lax.ppermute(own, "sector", [(i + 1, i) for i in range(sectors - 1)])
    got = lax.all_to_all(payload, "chain", 0, 0, tiled=True)
    env_out = kernel(
        scan_kernel,
        shape(segments, rows, rows),
        [HBM_SPEC] * 2,
        [
            pltpu.VMEM((rows, rows), F32),
            pltpu.VMEM((segments, 2 * rows, rows), BF16),
            pltpu.SemaphoreType.DMA,
            pltpu.SemaphoreType.DMA((4,)),
        ],
        flops=2 * 10**9,
    )(got, left_edge[0])
    env_out, early = lax.optimization_barrier((env_out, psi))
    env = lax.all_to_all(env_out, "chain", 0, 0, tiled=True)
    wide, mix, start, pairs = kernel(
        prepare_kernel,
        (
            shape(3, rows, rows * slots),
            shape(states * slots, deep),
            shape(rows * states, rows),
            shape(3, states, dtype=jnp.int32),
        ),
        [SMEM_SPEC] * 2 + [VMEM_SPEC] * 6,
        [
            pltpu.VMEM((3, rows * slots, rows), F32),
            pltpu.VMEM((rows * states, rows), F32),
            pltpu.SMEM((3,), jnp.int32),
        ],
        out_specs=(VMEM_SPEC,) * 3 + (SMEM_SPEC,),
        flops=5 * 10**9,
    )(charge_shift, block_size, below, own, above, early, operator, mpo_mask)
    chunk = 64
    stats, image = kernel(
        ham_kernel,
        (shape(sectors, 16, rows, dtype=F32), shape(ITERS, states, rows, rows)),
        [SMEM_SPEC] * 3 + [VMEM_SPEC] * 3 + [HBM_SPEC] * 2,
        [
            pltpu.VMEM((ITERS + 1, 8, rows), F32),
            pltpu.VMEM((rows * states, rows), F32),
            pltpu.VMEM((rows * states, rows), BF16),
            pltpu.VMEM((rows, channels * rows), BF16),
            pltpu.VMEM((chunk, deep, rows), BF16),
            pltpu.VMEM((states, rows * slots, rows), BF16),
            pltpu.VMEM((states, rows, rows), BF16),
            pltpu.VMEM((3, rows, rows * slots), BF16),
            pltpu.VMEM((ITERS, states, rows, rows), BF16),
            pltpu.SemaphoreType.DMA((2,)),
            pltpu.SemaphoreType.DMA((ITERS,)),
        ],
        out_specs=(VMEM_SPEC, HBM_SPEC),
        flops=10**10,
    )(charge_shift, block_size, pairs, env, mix, start, psi, wide)
    stats = lax.all_to_all(stats, "sector", 0, 0, tiled=True)
    out, energy = kernel(
        final_kernel,
        (shape(states, rows, rows), shape(1, dtype=F32)),
        [SMEM_SPEC] * 2 + [HBM_SPEC] * 3,
        [
            pltpu.VMEM(stats.shape, F32),
            pltpu.VMEM((states, rows, rows), BF16),
            pltpu.VMEM((ITERS, states, rows, rows), BF16),
            pltpu.VMEM((states, rows, rows), BF16),
            pltpu.SemaphoreType.DMA,
            pltpu.SemaphoreType.DMA((4, 2)),
            pltpu.SemaphoreType.DMA((4,)),
        ],
        out_specs=(HBM_SPEC, SMEM_SPEC),
        flops=10**7,
    )(charge_shift, block_size, stats, psi, image)
    return out[None, None], energy


def solution(mesh):
    placed = (
        P("sector", None, None, None),
        P("chain", "sector", None, None),
        P("chain", "sector", None, None, None),
        P("chain", "sector", None, None, None),
        P("chain", "sector", None, None, None),
        P(),
        P(),
        P("sector", None),
        P(),
    )
    return jax.shard_map(
        body,
        mesh=mesh,
        in_specs=placed,
        out_specs=(P("chain", "sector", None, None, None), P("chain")),
        check_vma=False,
    )
```

time: 112 us -> 97.4 us (0.87)
  blocking collectives: 42 us -> 20.1 us
  starting transfers between devices: 10.9 us -> 18.2 us
  waiting for transfers between devices: 8.89 us -> 14.5 us
  Pallas kernels: 45.2 us -> 42.3 us
  local copies, waits for them, and re-layouts: 3.48 us -> 0.81 us
    all_to_all x1 -> x0, blocking collectives: 23.9 us -> none  [body(): got = lax.all_to_all(payload, 'chain', 0, 0, tiled=True)]
    all_to_all x0 -> x1, waiting for transfers between devices: none -> 9.7 us  [body(): got = lax.all_to_all(payload, 'chain', 0, 0, tiled=True)]
    all_to_all x0 -> x1, starting transfers between devices: none -> 7.65 us  [body(): got = lax.all_to_all(payload, 'chain', 0, 0, tiled=True)]
    all_to_all x1, waiting for transfers between devices: 8.88 us -> 4.75 us  [body(): env = lax.all_to_all(env_out, 'chain', 0, 0, tiled=True)]
    pallas_call x4 -> x5, Pallas kernels: 45.2 us -> 42.3 us  [the longest x1 26.4 us: body(): kernel(ham_kernel, (shape(sectors, 16, rows, dtype=F32), shape(ITERS, sta...]
    unnamed x9 -> x4, local copies, waits for them, and re-layouts: 3.48 us -> 0.81 us
    all_to_all x1, blocking collectives: 18.1 us -> 20.1 us  [body(): stats = lax.all_to_all(stats, 'sector', 0, 0, tiled=True)]
  transfers between devices with their start and end apart: 3 -> 4, of which waited for: 1 -> 2; matrix products, arithmetic and copies ran while one was open for 2% -> 0% of each run, Pallas kernels for 0% -> 10%
where the time goes in v2:
time: 97.4 us; the launch traced here: 96.6 us
  Pallas kernels  42.3 us (43%)
  blocking collectives  20.1 us (21%)
  starting transfers between devices  18.2 us (19%)
  waiting for transfers between devices  14.5 us (15%)
    pallas_call x1, Pallas kernels, body(): kernel(ham_kernel, (shape(sectors, 16, rows, dtype=F32), shape(ITERS, sta...  26.4 us
    all_to_all x1, blocking collectives, body(): stats = lax.all_to_all(stats, 'sector', 0, 0, tiled=True)  20.1 us
    all_to_all x1, waiting for transfers between devices, body(): got = lax.all_to_all(payload, 'chain', 0, 0, tiled=True)  9.7 us
    all_to_all x1, starting transfers between devices, body(): got = lax.all_to_all(payload, 'chain', 0, 0, tiled=True)  7.65 us
    pallas_call x1, Pallas kernels, body(): kernel(prepare_kernel, (shape(3, rows, rows * slots), shape(states * slot...  4.99 us
    all_to_all x1, waiting for transfers between devices, body(): env = lax.all_to_all(env_out, 'chain', 0, 0, tiled=True)  4.75 us
    pallas_call x1, Pallas kernels, body(): kernel(scan_kernel, shape(segments, rows, rows), [HBM_SPEC] * 2, [pltpu.V...  4.53 us
    all_to_all x1, starting transfers between devices, body(): env = lax.all_to_all(env_out, 'chain', 0, 0, tiled=True)  4.21 us
  transfers between devices with their start and end apart: 4, of which 2 were waited for; matrix products, arithmetic and copies ran while one was open for 0% of the time, Pallas kernels for 10%

profile of v2, /device:TPU:1, one launch (start us, length us, event | category | flops | bytes accessed | tf_op | source)
XLA Modules:
  0.0 96.6 jit_solution(10843801950560219373)
XLA Ops:
  0.6 0.0 copy-start.1
  0.6 2.1 %shard_map.104 = bf16[16,256,128]{2,1,0:T(8,128)(2,1)} custom-call(f32[14,128,128]{2,1,0:T(8,128)} %bitcast.7, f32[128,128]{1,0:T(8,128)} %bitcast.11), custom_call_target="tpu_custom_call" | custom-call | flops 1000000 | bytes 4194304 | tf_op jit(solution)/shard_map/pallas_call | solution.py:424
  2.8 7.6 %all-to-all-start = ((bf16[16,256,128]{2,1,0:T(8,128)(2,1)}), bf16[16,256,128]{2,1,0:T(8,128)(2,1)}, u32[]{:S(2)}, u32[]{:S(2)}) async-start(bf16[16,256,128]{2,1,0:T(8,128)(2,1)} %shard_map.104), calls=%async_computation | async-start | bytes 2097152 | tf_op jit(solution)/shard_map/all_to_all | solution.py:440
  10.4 0.0 copy-done.1
  10.4 2.9 %collective-permute-start.1 = (bf16[14,128,128]{2,1,0:T(8,128)(2,1)S(1)}, bf16[14,128,128]{2,1,0:T(8,128)(2,1)}, u32[]{:S(2)}, u32[]{:S(2)}) collective-permute-start(bf16[14,128,128]{2,1,0:T(8,128)(2,1)S(1)} %bitcast.16), channel_id=1, source_target_pairs={{1,0},{2,1},{3,2},{4,3},{5,4},{6,5},{7,6},{8,7},{9,8},{10,9},{11,1... | collective-permute-start | bytes 1376264 | tf_op jit(solution)/shard_map/ppermute | solution.py:439
  13.3 3.4 %collective-permute-start = (bf16[14,128,128]{2,1,0:T(8,128)(2,1)S(1)}, bf16[14,128,128]{2,1,0:T(8,128)(2,1)}, u32[]{:S(2)}, u32[]{:S(2)}) collective-permute-start(bf16[14,128,128]{2,1,0:T(8,128)(2,1)S(1)} %bitcast.17), channel_id=1, source_target_pairs={{0,1},{1,2},{2,3},{3,4},{4,5},{5,6},{6,7},{7,8},{8,9},{9,10},{10,1... | collective-permute-start | bytes 1376264 | tf_op jit(solution)/shard_map/ppermute | solution.py:438
  16.8 9.7 %all-to-all-done.got_hbm = bf16[16,256,128]{2,1,0:T(8,128)(2,1)} async-done(((bf16[16,256,128]{2,1,0:T(8,128)(2,1)}), bf16[16,256,128]{2,1,0:T(8,128)(2,1)}, u32[]{:S(2)}, u32[]{:S(2)}) %all-to-all-start) | async-done | bytes 1048608 | tf_op jit(solution)/shard_map/all_to_all | solution.py:440
  26.5 4.5 %shard_map.105 = bf16[16,128,128]{2,1,0:T(8,128)(2,1)} custom-call(bf16[16,256,128]{2,1,0:T(8,128)(2,1)} %all-to-all-done.got_hbm, f32[14,128,128]{2,1,0:T(8,128)} %bitcast.12), custom_call_target="tpu_custom_call" | custom-call | flops 2000000000 | bytes 4194304 | tf_op jit(solution)/shard_map/pallas_call | solution.py:441
  31.0 4.2 %all-to-all-start.1 = ((bf16[16,128,128]{2,1,0:T(8,128)(2,1)}), bf16[16,128,128]{2,1,0:T(8,128)(2,1)S(1)}, u32[]{:S(2)}, u32[]{:S(2)}) async-start(bf16[16,128,128]{2,1,0:T(8,128)(2,1)} %shard_map.105), calls=%async_computation.1 | async-start | bytes 1048576 | tf_op jit(solution)/shard_map/all_to_all | solution.py:454
  35.2 0.0 collective-permute-done.1.above_ref
  35.2 0.0 collective-permute-done.below_ref
  35.2 5.0 %shard_map.106 = (bf16[3,128,2048]{2,1,0:T(8,128)(2,1)}, bf16[256,224]{1,0:T(8,128)(2,1)}, bf16[2048,128]{1,0:T(8,128)(2,1)}, s32[3,16]{1,0:T(4,128)}) custom-call(s32[1,16]{1,0:T(1,128)} %shift_ref.5, s32[16]{0:T(128)} %size_ref.5, bf16[14,128,128]{2,1,0:T(8,128)(2,1)} %collective-permute-done.below_ref, bf16[14,128,128]{2,1,0:T(8,128)(2,1)} %bitcast.15, ...), custom_call_target="tpu_custom_call" | custom-call | flops 5000000000 | bytes 4194304 | tf_op jit(solution)/shard_map/pallas_call | solution.py:455
  40.2 4.7 %all-to-all-done.1.env_ref = bf16[16,128,128]{2,1,0:T(8,128)(2,1)S(1)} async-done(((bf16[16,128,128]{2,1,0:T(8,128)(2,1)}), bf16[16,128,128]{2,1,0:T(8,128)(2,1)S(1)}, u32[]{:S(2)}, u32[]{:S(2)}) %all-to-all-start.1) | async-done | bytes 524320 | tf_op jit(solution)/shard_map/all_to_all | solution.py:454
  45.0 0.0 copy-start
  45.0 0.8 copy-done
  45.8 26.4 %shard_map.107 = (f32[16,16,128]{2,1,0:T(8,128)}, bf16[3,16,128,128]{3,2,1,0:T(8,128)(2,1)}) custom-call(s32[1,16]{1,0:T(1,128)} %shift_ref.5, s32[16]{0:T(128)} %size_ref.5, s32[3,16]{1,0:T(4,128)} %get-tuple-element.13.pair_ref, bf16[16,128,128]{2,1,0:T(8,128)(2,1)} %copy-done, bf16[256,224]{1,0:T(8,128)(2,1)} %get-tuple-element.15.mix_ref, ...), custom_call_target="tpu_custom_call" | custom-call | flops 10000000000 | bytes 4194304 | tf_op jit(solution)/shard_map/pallas_call | solution.py:473
  72.2 20.1 %all_to_all.15.stats_hbm = f32[16,16,128]{2,1,0:T(8,128)} all-to-all(f32[16,16,128]{2,1,0:T(8,128)} %get-tuple-element.18), channel_id=1, replica_groups=mesh['chain'=16,'sector'=16] {'sector'}, dimensions={0} | all-to-all | bytes 262144 | tf_op jit(solution)/shard_map/all_to_all | solution.py:493
  92.3 4.2 %shard_map.108 = (bf16[16,128,128]{2,1,0:T(8,128)(2,1)}, f32[1]{0:T(128)}) custom-call(s32[1,16]{1,0:T(1,128)} %shift_ref.5, s32[16]{0:T(128)} %size_ref.5, f32[16,16,128]{2,1,0:T(8,128)} %all_to_all.15.stats_hbm, bf16[16,128,128]{2,1,0:T(8,128)(2,1)} %bitcast.10, bf16[3,16,128,128]{3,2,1,0:T(8,128)(2,1)} %get-tuple-element.19.image_hbm), custom_call_target="tpu_custom_call" | custom-call | flops 10000000 | bytes 4194304 | tf_op jit(solution)/shard_map/pallas_call | solution.py:494
Async XLA Ops:
  0.6 9.8 %copy-start.1 = (bf16[1,1,14,128,128]{4,3,2,1,0:T(8,128)(2,1)S(1)}, bf16[1,1,14,128,128]{4,3,2,1,0:T(8,128)(2,1)}, u32[]{:S(2)}) copy-start(bf16[1,1,14,128,128]{4,3,2,1,0:T(8,128)(2,1)} %param.12) | copy-start | bytes 1376260
  2.8 23.7 %all-to-all-start = ((bf16[16,256,128]{2,1,0:T(8,128)(2,1)}), bf16[16,256,128]{2,1,0:T(8,128)(2,1)}, u32[]{:S(2)}, u32[]{:S(2)}) async-start(bf16[16,256,128]{2,1,0:T(8,128)(2,1)} %shard_map.104), calls=%async_computation | async-start | bytes 2097152 | tf_op jit(solution)/shard_map/all_to_all | solution.py:440
  10.4 24.8 %collective-permute-start.1 = (bf16[14,128,128]{2,1,0:T(8,128)(2,1)S(1)}, bf16[14,128,128]{2,1,0:T(8,128)(2,1)}, u32[]{:S(2)}, u32[]{:S(2)}) collective-permute-start(bf16[14,128,128]{2,1,0:T(8,128)(2,1)S(1)} %bitcast.16), channel_id=1, source_target_pairs={{1,0},{2,1},{3,2},{4,3},{5,4},{6,5},{7,6},{8,7},{9,8},{10,9},{11,1... | collective-permute-start | bytes 1376264 | tf_op jit(solution)/shard_map/ppermute | solution.py:439
  13.3 21.9 %collective-permute-start = (bf16[14,128,128]{2,1,0:T(8,128)(2,1)S(1)}, bf16[14,128,128]{2,1,0:T(8,128)(2,1)}, u32[]{:S(2)}, u32[]{:S(2)}) collective-permute-start(bf16[14,128,128]{2,1,0:T(8,128)(2,1)S(1)} %bitcast.17), channel_id=1, source_target_pairs={{0,1},{1,2},{2,3},{3,4},{4,5},{5,6},{6,7},{7,8},{8,9},{9,10},{10,1... | collective-permute-start | bytes 1376264 | tf_op jit(solution)/shard_map/ppermute | solution.py:438
  31.0 14.0 %all-to-all-start.1 = ((bf16[16,128,128]{2,1,0:T(8,128)(2,1)}), bf16[16,128,128]{2,1,0:T(8,128)(2,1)S(1)}, u32[]{:S(2)}, u32[]{:S(2)}) async-start(bf16[16,128,128]{2,1,0:T(8,128)(2,1)} %shard_map.105), calls=%async_computation.1 | async-start | bytes 1048576 | tf_op jit(solution)/shard_map/all_to_all | solution.py:454
  45.0 0.8 copy-start

commit v3 on v2

--- a/solution.py
+++ b/solution.py
@@ -217,8 +217,9 @@
 
 def ham_kernel(
     shift_ref, size_ref, pair_ref, env_ref, mix_ref, start_ref, psi_hbm, right_hbm,
-    stats_ref, image_hbm,
-    sums, vecs, unit, left, first, second, psi_ref, right_ref, image_ref, in_sems, image_sems,
+    stats_hbm, image_hbm,
+    stats_ref, sums, vecs, unit, left, first, second, psi_ref, right_ref, image_ref,
+    in_sems, image_sems,
 ):
     states, rows, _ = psi_ref.shape
     channels = mix_ref.shape[1] // states
@@ -315,28 +316,13 @@
     stats = jnp.concatenate(entries, axis=0)
     for s in range(stats_ref.shape[0]):
         stats_ref[s] = stats
+    stores.append(pltpu.make_async_copy(stats_ref, stats_hbm, image_sems.at[ITERS]))
+    stores[ITERS].start()
     for store in stores:
         store.wait()
 
 
-def final_kernel(
-    shift_ref, size_ref, stats_hbm, psi_hbm, image_hbm, out_hbm, energy_ref,
-    stats_ref, psi_ref, image_ref, out_ref, stats_sem, in_sems, out_sems,
-):
-    stats_fetch = pltpu.make_async_copy(stats_hbm, stats_ref, stats_sem)
-    stats_fetch.start()
-    groups = in_sems.shape[0]
-    fetches, stores = [], []
-    for n in range(groups):
-        part = pl.ds(n * psi_ref.shape[0] // groups, psi_ref.shape[0] // groups)
-        fetches.append(
-            pltpu.make_async_copy(image_hbm.at[:, part], image_ref.at[:, part], in_sems.at[n, 0])
-        )
-        fetches.append(pltpu.make_async_copy(psi_hbm.at[part], psi_ref.at[part], in_sems.at[n, 1]))
-        stores.append(pltpu.make_async_copy(out_ref.at[part], out_hbm.at[part], out_sems.at[n]))
-    for fetch in fetches:
-        fetch.start()
-    stats_fetch.wait()
+def final_kernel(shift_ref, size_ref, stats_ref, psi_ref, image_ref, out_ref, energy_ref):
     q = lax.axis_index("sector")
     sectors, _, rows = stats_ref.shape
     states = psi_ref.shape[0]
@@ -376,19 +362,12 @@
     col_id = lax.broadcasted_iota(jnp.int32, (rows, rows), 1)
     own_size = size_ref[q]
     for p in range(states):
-        if p % (states // groups) == 0:
-            fetches[2 * (p * groups // states)].wait()
-            fetches[2 * (p * groups // states) + 1].wait()
         limit = slot_limit(q, shift_ref[0, p], size_ref)
         live = jnp.logical_and(col_id < limit, row_id < own_size)
         total = own[0] * jnp.where(live, psi_ref[p].astype(F32), 0.0)
         for k in range(ITERS):
             total = total + own[k + 1] * image_ref[k, p].astype(F32)
         out_ref[p] = total.astype(BF16)
-        if (p + 1) % (states // groups) == 0:
-            stores[p * groups // states].start()
-    for store in stores:
-        store.wait()
 
 
 def body(
@@ -475,6 +454,7 @@
         (shape(sectors, 16, rows, dtype=F32), shape(ITERS, states, rows, rows)),
         [SMEM_SPEC] * 3 + [VMEM_SPEC] * 3 + [HBM_SPEC] * 2,
         [
+            pltpu.VMEM((sectors, 16, rows), F32),
             pltpu.VMEM((ITERS + 1, 8, rows), F32),
             pltpu.VMEM((rows * states, rows), F32),
             pltpu.VMEM((rows * states, rows), BF16),
@@ -485,26 +465,18 @@
             pltpu.VMEM((3, rows, rows * slots), BF16),
             pltpu.VMEM((ITERS, states, rows, rows), BF16),
             pltpu.SemaphoreType.DMA((2,)),
-            pltpu.SemaphoreType.DMA((ITERS,)),
+            pltpu.SemaphoreType.DMA((ITERS + 1,)),
         ],
-        out_specs=(VMEM_SPEC, HBM_SPEC),
+        out_specs=(HBM_SPEC, HBM_SPEC),
         flops=10**10,
     )(charge_shift, block_size, pairs, env, mix, start, psi, wide)
     stats = lax.all_to_all(stats, "sector", 0, 0, tiled=True)
     out, energy = kernel(
         final_kernel,
         (shape(states, rows, rows), shape(1, dtype=F32)),
-        [SMEM_SPEC] * 2 + [HBM_SPEC] * 3,
-        [
-            pltpu.VMEM(stats.shape, F32),
-            pltpu.VMEM((states, rows, rows), BF16),
-            pltpu.VMEM((ITERS, states, rows, rows), BF16),
-            pltpu.VMEM((states, rows, rows), BF16),
-            pltpu.SemaphoreType.DMA,
-            pltpu.SemaphoreType.DMA((4, 2)),
-            pltpu.SemaphoreType.DMA((4,)),
-        ],
-        out_specs=(HBM_SPEC, SMEM_SPEC),
+        [SMEM_SPEC] * 2 + [VMEM_SPEC] * 3,
+        [],
+        out_specs=(VMEM_SPEC, SMEM_SPEC),
         flops=10**7,
     )(charge_shift, block_size, stats, psi, image)
     return out[None, None], energy

time: 97.4 us -> 95.9 us (0.985)
  Pallas kernels: 42.3 us -> 39.3 us
  blocking collectives: 20.1 us -> 21.8 us
    pallas_call x1, Pallas kernels: 26.4 us -> 24.6 us  [body(): kernel(ham_kernel, (shape(sectors, 16, rows, dtype=F32), shape(ITERS, sta...]
    all_to_all x1, blocking collectives: 20.1 us -> 21.8 us  [body(): stats = lax.all_to_all(stats, 'sector', 0, 0, tiled=True)]
    pallas_call x1, Pallas kernels: 4.16 us -> 3.08 us  [body(): kernel(final_kernel, (shape(states, rows, rows), shape(1, dtype=F32)), [S...]
where the time goes in v3:
time: 95.9 us; the launch traced here: 95.4 us
  Pallas kernels  39.3 us (41%)
  blocking collectives  21.8 us (23%)
  starting transfers between devices  18.2 us (19%)
  waiting for transfers between devices  14.5 us (15%)
    pallas_call x1, Pallas kernels, body(): kernel(ham_kernel, (shape(sectors, 16, rows, dtype=F32), shape(ITERS, sta...  24.6 us
    all_to_all x1, blocking collectives, body(): stats = lax.all_to_all(stats, 'sector', 0, 0, tiled=True)  21.8 us
    all_to_all x1, waiting for transfers between devices, body(): got = lax.all_to_all(payload, 'chain', 0, 0, tiled=True)  9.7 us
    all_to_all x1, starting transfers between devices, body(): got = lax.all_to_all(payload, 'chain', 0, 0, tiled=True)  7.65 us
    pallas_call x1, Pallas kernels, body(): kernel(prepare_kernel, (shape(3, rows, rows * slots), shape(states * slot...  4.99 us
    all_to_all x1, waiting for transfers between devices, body(): env = lax.all_to_all(env_out, 'chain', 0, 0, tiled=True)  4.75 us
    pallas_call x1, Pallas kernels, body(): kernel(scan_kernel, shape(segments, rows, rows), [HBM_SPEC] * 2, [pltpu.V...  4.53 us
    all_to_all x1, starting transfers between devices, body(): env = lax.all_to_all(env_out, 'chain', 0, 0, tiled=True)  4.21 us
  transfers between devices with their start and end apart: 4, of which 2 were waited for; matrix products, arithmetic and copies ran while one was open for 0% of the time, Pallas kernels for 10%

profile of v3, /device:TPU:1, one launch (start us, length us, event | category | flops | bytes accessed | tf_op | source)
XLA Modules:
  0.0 95.4 jit_solution(16188716276570354599)
XLA Ops:
  0.6 0.0 copy-start.1
  0.6 2.1 %shard_map.104 = bf16[16,256,128]{2,1,0:T(8,128)(2,1)} custom-call(f32[14,128,128]{2,1,0:T(8,128)} %bitcast.7, f32[128,128]{1,0:T(8,128)} %bitcast.11), custom_call_target="tpu_custom_call" | custom-call | flops 1000000 | bytes 4194304 | tf_op jit(solution)/shard_map/pallas_call | solution.py:403
  2.8 7.6 %all-to-all-start = ((bf16[16,256,128]{2,1,0:T(8,128)(2,1)}), bf16[16,256,128]{2,1,0:T(8,128)(2,1)}, u32[]{:S(2)}, u32[]{:S(2)}) async-start(bf16[16,256,128]{2,1,0:T(8,128)(2,1)} %shard_map.104), calls=%async_computation | async-start | bytes 2097152 | tf_op jit(solution)/shard_map/all_to_all | solution.py:419
  10.4 0.0 copy-done.1
  10.4 2.9 %collective-permute-start.1 = (bf16[14,128,128]{2,1,0:T(8,128)(2,1)S(1)}, bf16[14,128,128]{2,1,0:T(8,128)(2,1)}, u32[]{:S(2)}, u32[]{:S(2)}) collective-permute-start(bf16[14,128,128]{2,1,0:T(8,128)(2,1)S(1)} %bitcast.16), channel_id=1, source_target_pairs={{1,0},{2,1},{3,2},{4,3},{5,4},{6,5},{7,6},{8,7},{9,8},{10,9},{11,1... | collective-permute-start | bytes 1376264 | tf_op jit(solution)/shard_map/ppermute | solution.py:418
  13.3 3.4 %collective-permute-start = (bf16[14,128,128]{2,1,0:T(8,128)(2,1)S(1)}, bf16[14,128,128]{2,1,0:T(8,128)(2,1)}, u32[]{:S(2)}, u32[]{:S(2)}) collective-permute-start(bf16[14,128,128]{2,1,0:T(8,128)(2,1)S(1)} %bitcast.17), channel_id=1, source_target_pairs={{0,1},{1,2},{2,3},{3,4},{4,5},{5,6},{6,7},{7,8},{8,9},{9,10},{10,1... | collective-permute-start | bytes 1376264 | tf_op jit(solution)/shard_map/ppermute | solution.py:417
  16.8 9.7 %all-to-all-done.got_hbm = bf16[16,256,128]{2,1,0:T(8,128)(2,1)} async-done(((bf16[16,256,128]{2,1,0:T(8,128)(2,1)}), bf16[16,256,128]{2,1,0:T(8,128)(2,1)}, u32[]{:S(2)}, u32[]{:S(2)}) %all-to-all-start) | async-done | bytes 1048608 | tf_op jit(solution)/shard_map/all_to_all | solution.py:419
  26.5 4.5 %shard_map.105 = bf16[16,128,128]{2,1,0:T(8,128)(2,1)} custom-call(bf16[16,256,128]{2,1,0:T(8,128)(2,1)} %all-to-all-done.got_hbm, f32[14,128,128]{2,1,0:T(8,128)} %bitcast.12), custom_call_target="tpu_custom_call" | custom-call | flops 2000000000 | bytes 4194304 | tf_op jit(solution)/shard_map/pallas_call | solution.py:420
  31.0 4.2 %all-to-all-start.1 = ((bf16[16,128,128]{2,1,0:T(8,128)(2,1)}), bf16[16,128,128]{2,1,0:T(8,128)(2,1)S(1)}, u32[]{:S(2)}, u32[]{:S(2)}) async-start(bf16[16,128,128]{2,1,0:T(8,128)(2,1)} %shard_map.105), calls=%async_computation.1 | async-start | bytes 1048576 | tf_op jit(solution)/shard_map/all_to_all | solution.py:433
  35.2 0.0 collective-permute-done.1.above_ref
  35.2 0.0 collective-permute-done.below_ref
  35.2 5.0 %shard_map.106 = (bf16[3,128,2048]{2,1,0:T(8,128)(2,1)}, bf16[256,224]{1,0:T(8,128)(2,1)}, bf16[2048,128]{1,0:T(8,128)(2,1)}, s32[3,16]{1,0:T(4,128)}) custom-call(s32[1,16]{1,0:T(1,128)} %shift_ref.5, s32[16]{0:T(128)} %size_ref.5, bf16[14,128,128]{2,1,0:T(8,128)(2,1)} %collective-permute-done.below_ref, bf16[14,128,128]{2,1,0:T(8,128)(2,1)} %bitcast.15, ...), custom_call_target="tpu_custom_call" | custom-call | flops 5000000000 | bytes 4194304 | tf_op jit(solution)/shard_map/pallas_call | solution.py:434
  40.2 4.7 %all-to-all-done.1.env_ref = bf16[16,128,128]{2,1,0:T(8,128)(2,1)S(1)} async-done(((bf16[16,128,128]{2,1,0:T(8,128)(2,1)}), bf16[16,128,128]{2,1,0:T(8,128)(2,1)S(1)}, u32[]{:S(2)}, u32[]{:S(2)}) %all-to-all-start.1) | async-done | bytes 524320 | tf_op jit(solution)/shard_map/all_to_all | solution.py:433
  45.0 0.0 copy-start
  45.0 0.8 copy-done
  45.8 24.6 %shard_map.107 = (f32[16,16,128]{2,1,0:T(8,128)}, bf16[3,16,128,128]{3,2,1,0:T(8,128)(2,1)}) custom-call(s32[1,16]{1,0:T(1,128)} %shift_ref.5, s32[16]{0:T(128)} %size_ref.5, s32[3,16]{1,0:T(4,128)} %get-tuple-element.13.pair_ref, bf16[16,128,128]{2,1,0:T(8,128)(2,1)} %copy-done, bf16[256,224]{1,0:T(8,128)(2,1)} %get-tuple-element.15.mix_ref, ...), custom_call_target="tpu_custom_call" | custom-call | flops 10000000000 | bytes 4194304 | tf_op jit(solution)/shard_map/pallas_call | solution.py:452
  70.4 21.8 %all_to_all.15.stats_ref = f32[16,16,128]{2,1,0:T(8,128)} all-to-all(f32[16,16,128]{2,1,0:T(8,128)} %get-tuple-element.18), channel_id=1, replica_groups=mesh['chain'=16,'sector'=16] {'sector'}, dimensions={0} | all-to-all | bytes 262144 | tf_op jit(solution)/shard_map/all_to_all | solution.py:473
  92.2 3.1 %shard_map.108 = (bf16[16,128,128]{2,1,0:T(8,128)(2,1)}, f32[1]{0:T(128)}) custom-call(s32[1,16]{1,0:T(1,128)} %shift_ref.5, s32[16]{0:T(128)} %size_ref.5, f32[16,16,128]{2,1,0:T(8,128)} %all_to_all.15.stats_ref, bf16[16,128,128]{2,1,0:T(8,128)(2,1)} %bitcast.10, bf16[3,16,128,128]{3,2,1,0:T(8,128)(2,1)} %get-tuple-element.19.image_ref), custom_call_target="tpu_custom_call" | custom-call | flops 10000000 | bytes 4194304 | tf_op jit(solution)/shard_map/pallas_call | solution.py:474
Async XLA Ops:
  0.6 9.8 %copy-start.1 = (bf16[1,1,14,128,128]{4,3,2,1,0:T(8,128)(2,1)S(1)}, bf16[1,1,14,128,128]{4,3,2,1,0:T(8,128)(2,1)}, u32[]{:S(2)}) copy-start(bf16[1,1,14,128,128]{4,3,2,1,0:T(8,128)(2,1)} %param.12) | copy-start | bytes 1376260
  2.8 23.7 %all-to-all-start = ((bf16[16,256,128]{2,1,0:T(8,128)(2,1)}), bf16[16,256,128]{2,1,0:T(8,128)(2,1)}, u32[]{:S(2)}, u32[]{:S(2)}) async-start(bf16[16,256,128]{2,1,0:T(8,128)(2,1)} %shard_map.104), calls=%async_computation | async-start | bytes 2097152 | tf_op jit(solution)/shard_map/all_to_all | solution.py:419
  10.4 24.8 %collective-permute-start.1 = (bf16[14,128,128]{2,1,0:T(8,128)(2,1)S(1)}, bf16[14,128,128]{2,1,0:T(8,128)(2,1)}, u32[]{:S(2)}, u32[]{:S(2)}) collective-permute-start(bf16[14,128,128]{2,1,0:T(8,128)(2,1)S(1)} %bitcast.16), channel_id=1, source_target_pairs={{1,0},{2,1},{3,2},{4,3},{5,4},{6,5},{7,6},{8,7},{9,8},{10,9},{11,1... | collective-permute-start | bytes 1376264 | tf_op jit(solution)/shard_map/ppermute | solution.py:418
  13.3 21.9 %collective-permute-start = (bf16[14,128,128]{2,1,0:T(8,128)(2,1)S(1)}, bf16[14,128,128]{2,1,0:T(8,128)(2,1)}, u32[]{:S(2)}, u32[]{:S(2)}) collective-permute-start(bf16[14,128,128]{2,1,0:T(8,128)(2,1)S(1)} %bitcast.17), channel_id=1, source_target_pairs={{0,1},{1,2},{2,3},{3,4},{4,5},{5,6},{6,7},{7,8},{8,9},{9,10},{10,1... | collective-permute-start | bytes 1376264 | tf_op jit(solution)/shard_map/ppermute | solution.py:417
  31.0 14.0 %all-to-all-start.1 = ((bf16[16,128,128]{2,1,0:T(8,128)(2,1)}), bf16[16,128,128]{2,1,0:T(8,128)(2,1)S(1)}, u32[]{:S(2)}, u32[]{:S(2)}) async-start(bf16[16,128,128]{2,1,0:T(8,128)(2,1)} %shard_map.105), calls=%async_computation.1 | async-start | bytes 1048576 | tf_op jit(solution)/shard_map/all_to_all | solution.py:433
  45.0 0.8 copy-start

commit v4 on v3

--- a/solution.py
+++ b/solution.py
@@ -12,8 +12,6 @@
 STEP = 0.5
 F32 = jnp.float32
 BF16 = jnp.bfloat16
-VMEM_LIMIT = 63 * 2**20
-
 SMEM_SPEC = pl.BlockSpec(memory_space=pltpu.SMEM)
 VMEM_SPEC = pl.BlockSpec(memory_space=pltpu.VMEM)
 HBM_SPEC = pl.BlockSpec(memory_space=pltpu.HBM)
@@ -381,7 +379,7 @@
     own, psi = right_env[0, 0], psi_init[0, 0]
     operator = jnp.transpose(mpo, (0, 3, 1, 2))
 
-    def kernel(function, out_shape, in_specs, scratch, out_specs=None, flops=0, grid=()):
+    def kernel(function, out_shape, in_specs, scratch, out_specs=None, flops=0, mib=63, grid=()):
         shapes = out_shape if isinstance(out_shape, tuple) else (out_shape,)
         specs = out_specs or tuple(VMEM_SPEC for _ in shapes)
         return pl.pallas_call(
@@ -391,7 +389,7 @@
             in_specs=in_specs,
             out_specs=specs if isinstance(out_shape, tuple) else specs[0],
             scratch_shapes=scratch,
-            compiler_params=pltpu.CompilerParams(vmem_limit_bytes=VMEM_LIMIT),
+            compiler_params=pltpu.CompilerParams(vmem_limit_bytes=mib * 2**20),
             cost_estimate=pl.CostEstimate(
                 flops=flops, bytes_accessed=4 * 2**20, transcendentals=0
             ),
@@ -428,6 +426,7 @@
             pltpu.SemaphoreType.DMA((4,)),
         ],
         flops=2 * 10**9,
+        mib=40,
     )(got, left_edge[0])
     env_out, early = lax.optimization_barrier((env_out, psi))
     env = lax.all_to_all(env_out, "chain", 0, 0, tiled=True)
@@ -447,6 +446,7 @@
         ],
         out_specs=(VMEM_SPEC,) * 3 + (SMEM_SPEC,),
         flops=5 * 10**9,
+        mib=40,
     )(charge_shift, block_size, below, own, above, early, operator, mpo_mask)
     chunk = 64
     stats, image = kernel(
@@ -469,6 +469,7 @@
         ],
         out_specs=(HBM_SPEC, HBM_SPEC),
         flops=10**10,
+        mib=40,
     )(charge_shift, block_size, pairs, env, mix, start, psi, wide)
     stats = lax.all_to_all(stats, "sector", 0, 0, tiled=True)
     out, energy = kernel(
@@ -478,6 +479,7 @@
         [],
         out_specs=(VMEM_SPEC, SMEM_SPEC),
         flops=10**7,
+        mib=16,
     )(charge_shift, block_size, stats, psi, image)
     return out[None, None], energy
 

time: 95.9 us -> 92.7 us (0.967)
  Pallas kernels: 39.3 us -> 35.5 us
  local copies, waits for them, and re-layouts: 0.81 us -> 2.61 us
    unnamed x4 -> x16, local copies, waits for them, and re-layouts: 0.81 us -> 2.61 us
    pallas_call x1, Pallas kernels: 3.08 us -> 2 us  [body(): kernel(final_kernel, (shape(states, rows, rows), shape(1, dtype=F32)), [S...]
    pallas_call x1, Pallas kernels: 4.53 us -> 3.52 us  [body(): kernel(scan_kernel, shape(segments, rows, rows), [HBM_SPEC] * 2, [pltpu.V...]
  transfers between devices with their start and end apart: 4 -> 4, of which waited for: 2 -> 2; matrix products, arithmetic and copies ran while one was open for 0% -> 0% of each run, Pallas kernels for 10% -> 8%
where the time goes in v4:
time: 92.7 us
  Pallas kernels  35.5 us (38%)
  blocking collectives  21.4 us (23%)
  starting transfers between devices  18.1 us (20%)
  waiting for transfers between devices  14.1 us (15%)
  local copies, waits for them, and re-layouts  2.61 us (3%)
  between operations  0.95 us (1%)
    pallas_call x1, Pallas kernels, body(): kernel(ham_kernel, (shape(sectors, 16, rows, dtype=F32), shape(ITERS, sta...  23.8 us
    all_to_all x1, blocking collectives, body(): stats = lax.all_to_all(stats, 'sector', 0, 0, tiled=True)  21.4 us
    all_to_all x1, waiting for transfers between devices, body(): got = lax.all_to_all(payload, 'chain', 0, 0, tiled=True)  9.66 us
    all_to_all x1, starting transfers between devices, body(): got = lax.all_to_all(payload, 'chain', 0, 0, tiled=True)  7.6 us
    all_to_all x1, waiting for transfers between devices, body(): env = lax.all_to_all(env_out, 'chain', 0, 0, tiled=True)  4.46 us
    all_to_all x1, starting transfers between devices, body(): env = lax.all_to_all(env_out, 'chain', 0, 0, tiled=True)  4.21 us
    pallas_call x1, Pallas kernels, body(): kernel(prepare_kernel, (shape(3, rows, rows * slots), shape(states * slot...  4.05 us
    pallas_call x1, Pallas kernels, body(): kernel(scan_kernel, shape(segments, rows, rows), [HBM_SPEC] * 2, [pltpu.V...  3.52 us
  transfers between devices with their start and end apart: 4, of which 2 were waited for; matrix products, arithmetic and copies ran while one was open for 0% of the time, Pallas kernels for 8%

profile of v4, /device:TPU:1, one launch (start us, length us, event | category | flops | bytes accessed | tf_op | source)
XLA Modules:
  0.0 92.7 jit_solution(760228056928542587)
XLA Ops:
  0.6 0.0 copy-start.3
  0.6 2.2 %shard_map.104 = bf16[16,256,128]{2,1,0:T(8,128)(2,1)} custom-call(f32[14,128,128]{2,1,0:T(8,128)} %bitcast.12, f32[128,128]{1,0:T(8,128)} %bitcast.13), custom_call_target="tpu_custom_call" | custom-call | flops 1000000 | bytes 4194304 | tf_op jit(solution)/shard_map/pallas_call | solution.py:401
  2.8 7.6 %all-to-all-start = ((bf16[16,256,128]{2,1,0:T(8,128)(2,1)}), bf16[16,256,128]{2,1,0:T(8,128)(2,1)S(1)}, u32[]{:S(2)}, u32[]{:S(2)}) async-start(bf16[16,256,128]{2,1,0:T(8,128)(2,1)} %shard_map.104), calls=%async_computation | async-start | bytes 2097152 | tf_op jit(solution)/shard_map/all_to_all | solution.py:417
  10.4 2.9 %collective-permute-start.1 = (bf16[14,128,128]{2,1,0:T(8,128)(2,1)}, bf16[14,128,128]{2,1,0:T(8,128)(2,1)}, u32[]{:S(2)}, u32[]{:S(2)}) collective-permute-start(bf16[14,128,128]{2,1,0:T(8,128)(2,1)} %bitcast.own_ref), channel_id=1, source_target_pairs={{1,0},{2,1},{3,2},{4,3},{5,4},{6,5},{7,6},{8,7},{9,8},{10,9},{11,1... | collective-permute-start | bytes 1376264 | tf_op jit(solution)/shard_map/ppermute | solution.py:416
  13.3 3.4 %collective-permute-start = (bf16[14,128,128]{2,1,0:T(8,128)(2,1)}, bf16[14,128,128]{2,1,0:T(8,128)(2,1)}, u32[]{:S(2)}, u32[]{:S(2)}) collective-permute-start(bf16[14,128,128]{2,1,0:T(8,128)(2,1)} %bitcast.own_ref), channel_id=1, source_target_pairs={{0,1},{1,2},{2,3},{3,4},{4,5},{5,6},{6,7},{7,8},{8,9},{9,10},{10,1... | collective-permute-start | bytes 1376264 | tf_op jit(solution)/shard_map/ppermute | solution.py:415
  16.7 9.7 %all-to-all-done.got_hbm = bf16[16,256,128]{2,1,0:T(8,128)(2,1)S(1)} async-done(((bf16[16,256,128]{2,1,0:T(8,128)(2,1)}), bf16[16,256,128]{2,1,0:T(8,128)(2,1)S(1)}, u32[]{:S(2)}, u32[]{:S(2)}) %all-to-all-start) | async-done | bytes 1048608 | tf_op jit(solution)/shard_map/all_to_all | solution.py:417
  26.4 0.0 copy-start.4
  26.4 0.0 copy-start.5
  26.4 3.5 %shard_map.105 = bf16[16,128,128]{2,1,0:T(8,128)(2,1)} custom-call(bf16[16,256,128]{2,1,0:T(8,128)(2,1)S(1)} %all-to-all-done.got_hbm, f32[14,128,128]{2,1,0:T(8,128)S(1)} %bitcast.10), custom_call_target="tpu_custom_call" | custom-call | flops 2000000000 | bytes 4194304 | tf_op jit(solution)/shard_map/pallas_call | solution.py:418
  30.0 4.2 %all-to-all-start.1 = ((bf16[16,128,128]{2,1,0:T(8,128)(2,1)}), bf16[16,128,128]{2,1,0:T(8,128)(2,1)S(1)}, u32[]{:S(2)}, u32[]{:S(2)}) async-start(bf16[16,128,128]{2,1,0:T(8,128)(2,1)} %shard_map.105), calls=%async_computation.1 | async-start | bytes 1048576 | tf_op jit(solution)/shard_map/all_to_all | solution.py:432
  34.2 0.0 collective-permute-done.1.above_ref
  34.2 0.0 collective-permute-done.below_ref
  34.2 0.0 copy-done
  34.2 0.0 copy-done.1
  34.2 0.0 copy-done.2
  34.2 0.0 copy-done.4
  34.2 0.0 copy-done.5
  34.2 4.0 %shard_map.106 = (bf16[3,128,2048]{2,1,0:T(8,128)(2,1)S(1)}, bf16[256,224]{1,0:T(8,128)(2,1)S(1)}, bf16[2048,128]{1,0:T(8,128)(2,1)S(1)}, s32[3,16]{1,0:T(4,128)S(1)}) custom-call(s32[1,16]{1,0:T(1,128)S(1)} %copy-done.1, s32[16]{0:T(128)S(1)} %copy-done.2, bf16[14,128,128]{2,1,0:T(8,128)(2,1)} %collective-permute-done.below_ref, ...), custom_call_target="tpu_custom_call" | custom-call | flops 5000000000 | bytes 4194304 | tf_op jit(solution)/shard_map/pallas_call | solution.py:433
  38.3 1.2 %copy-done.6 = bf16[3,128,2048]{2,1,0:T(8,128)(2,1)} copy-done((bf16[3,128,2048]{2,1,0:T(8,128)(2,1)}, bf16[3,128,2048]{2,1,0:T(8,128)(2,1)S(1)}, u32[]{:S(2)}) %copy-start.6) | copy-done | bytes 1572888
  39.5 4.5 %all-to-all-done.1.env_ref = bf16[16,128,128]{2,1,0:T(8,128)(2,1)S(1)} async-done(((bf16[16,128,128]{2,1,0:T(8,128)(2,1)}), bf16[16,128,128]{2,1,0:T(8,128)(2,1)S(1)}, u32[]{:S(2)}, u32[]{:S(2)}) %all-to-all-start.1) | async-done | bytes 524320 | tf_op jit(solution)/shard_map/all_to_all | solution.py:432
  43.9 1.4 %copy-done.7 = bf16[3,128,2048]{2,1,0:T(8,128)(2,1)S(1)} copy-done((bf16[3,128,2048]{2,1,0:T(8,128)(2,1)S(1)}, bf16[3,128,2048]{2,1,0:T(8,128)(2,1)}, u32[]{:S(2)}) %copy-start.7) | copy-done | bytes 1572888
  45.4 23.8 %shard_map.107 = (f32[16,16,128]{2,1,0:T(8,128)S(1)}, bf16[3,16,128,128]{3,2,1,0:T(8,128)(2,1)S(1)}) custom-call(s32[1,16]{1,0:T(1,128)S(1)} %copy-done.1, s32[16]{0:T(128)S(1)} %copy-done.2, s32[3,16]{1,0:T(4,128)S(1)} %get-tuple-element.13.pair_ref, bf16[16,128,128]{2,1,0:T(8,128)(2,1)S(1)} %all-to-all-done.1.env_ref, ...), custom_call_target="tpu_custom_call" | custom-call | flops 10000000000 | bytes 4194304 | tf_op jit(solution)/shard_map/pallas_call | solution.py:452
  69.1 21.4 %all_to_all.15.stats_ref = f32[16,16,128]{2,1,0:T(8,128)S(1)} all-to-all(f32[16,16,128]{2,1,0:T(8,128)S(1)} %get-tuple-element.18), channel_id=1, replica_groups=mesh['chain'=16,'sector'=16] {'sector'}, dimensions={0} | all-to-all | bytes 262144 | tf_op jit(solution)/shard_map/all_to_all | solution.py:474
  90.6 2.0 %shard_map.108 = (bf16[16,128,128]{2,1,0:T(8,128)(2,1)}, f32[1]{0:T(128)}) custom-call(s32[1,16]{1,0:T(1,128)S(1)} %copy-done.1, s32[16]{0:T(128)S(1)} %copy-done.2, f32[16,16,128]{2,1,0:T(8,128)S(1)} %all_to_all.15.stats_ref, bf16[16,128,128]{2,1,0:T(8,128)(2,1)S(1)} %bitcast.9, bf16[3,16,128,128]{3,2,1,0:T(8,128)(2,1)S(1)} %get-tuple-element.19.image_ref), custom_call_target="tpu_custom_call" | custom-call | flops 10000000 | bytes 4194304 | tf_op jit(solution)/shard_map/pallas_call | solution.py:475
  (6 shorter events, 0.0 us)
Async XLA Ops:
  0.6 25.8 %copy-start.3 = (f32[1,14,128,128]{3,2,1,0:T(8,128)S(1)}, f32[1,14,128,128]{3,2,1,0:T(8,128)}, u32[]{:S(2)}) copy-start(f32[1,14,128,128]{3,2,1,0:T(8,128)} %param.9) | copy-start | bytes 2752516
  2.8 23.6 %all-to-all-start = ((bf16[16,256,128]{2,1,0:T(8,128)(2,1)}), bf16[16,256,128]{2,1,0:T(8,128)(2,1)S(1)}, u32[]{:S(2)}, u32[]{:S(2)}) async-start(bf16[16,256,128]{2,1,0:T(8,128)(2,1)} %shard_map.104), calls=%async_computation | async-start | bytes 2097152 | tf_op jit(solution)/shard_map/all_to_all | solution.py:417
  10.4 23.8 %collective-permute-start.1 = (bf16[14,128,128]{2,1,0:T(8,128)(2,1)}, bf16[14,128,128]{2,1,0:T(8,128)(2,1)}, u32[]{:S(2)}, u32[]{:S(2)}) collective-permute-start(bf16[14,128,128]{2,1,0:T(8,128)(2,1)} %bitcast.own_ref), channel_id=1, source_target_pairs={{1,0},{2,1},{3,2},{4,3},{5,4},{6,5},{7,6},{8,7},{9,8},{10,9},{11,1... | collective-permute-start | bytes 1376264 | tf_op jit(solution)/shard_map/ppermute | solution.py:416
  13.3 20.9 %collective-permute-start = (bf16[14,128,128]{2,1,0:T(8,128)(2,1)}, bf16[14,128,128]{2,1,0:T(8,128)(2,1)}, u32[]{:S(2)}, u32[]{:S(2)}) collective-permute-start(bf16[14,128,128]{2,1,0:T(8,128)(2,1)} %bitcast.own_ref), channel_id=1, source_target_pairs={{0,1},{1,2},{2,3},{3,4},{4,5},{5,6},{6,7},{7,8},{8,9},{9,10},{10,1... | collective-permute-start | bytes 1376264 | tf_op jit(solution)/shard_map/ppermute | solution.py:415
  26.4 7.8 %copy-start = (bf16[1,1,16,128,128]{4,3,2,1,0:T(8,128)(2,1)S(1)}, bf16[1,1,16,128,128]{4,3,2,1,0:T(8,128)(2,1)}, u32[]{:S(2)}) copy-start(bf16[1,1,16,128,128]{4,3,2,1,0:T(8,128)(2,1)} %param.13) | copy-start | bytes 1572868
  26.4 7.8 %copy-start.1 = (s32[1,16]{1,0:T(1,128)S(1)}, s32[1,16]{1,0:T(1,128)}, u32[]{:S(2)}) copy-start(s32[1,16]{1,0:T(1,128)} %shift_ref.5) | copy-start | bytes 196
  26.4 7.8 %copy-start.2 = (s32[16]{0:T(128)S(1)}, s32[16]{0:T(128)}, u32[]{:S(2)}) copy-start(s32[16]{0:T(128)} %size_ref.5) | copy-start | bytes 196
  26.4 7.8 %copy-start.4 = (bf16[14,16,16,14]{2,1,3,0:T(8,128)(2,1)S(1)}, bf16[14,16,16,14]{2,1,3,0:T(8,128)(2,1)}, u32[]{:S(2)}) copy-start(bf16[14,16,16,14]{2,1,3,0:T(8,128)(2,1)} %param.14) | copy-start | bytes 301060
  26.4 7.8 %copy-start.5 = (s32[14,14]{1,0:T(8,128)S(1)}, s32[14,14]{1,0:T(8,128)}, u32[]{:S(2)}) copy-start(s32[14,14]{1,0:T(8,128)} %chan_ref.1) | copy-start | bytes 2356
  30.0 14.0 %all-to-all-start.1 = ((bf16[16,128,128]{2,1,0:T(8,128)(2,1)}), bf16[16,128,128]{2,1,0:T(8,128)(2,1)S(1)}, u32[]{:S(2)}, u32[]{:S(2)}) async-start(bf16[16,128,128]{2,1,0:T(8,128)(2,1)} %shard_map.105), calls=%async_computation.1 | async-start | bytes 1048576 | tf_op jit(solution)/shard_map/all_to_all | solution.py:432
  38.3 1.2 %copy-start.6 = (bf16[3,128,2048]{2,1,0:T(8,128)(2,1)}, bf16[3,128,2048]{2,1,0:T(8,128)(2,1)S(1)}, u32[]{:S(2)}) copy-start(bf16[3,128,2048]{2,1,0:T(8,128)(2,1)S(1)} %get-tuple-element.17.right_hbm) | copy-start | bytes 4718596
  43.9 1.4 %copy-start.7 = (bf16[3,128,2048]{2,1,0:T(8,128)(2,1)S(1)}, bf16[3,128,2048]{2,1,0:T(8,128)(2,1)}, u32[]{:S(2)}) copy-start(bf16[3,128,2048]{2,1,0:T(8,128)(2,1)} %copy-done.6) | copy-start | bytes 4718596
